TPU v7x, 256 devices: a whole 4x4x8 slice. The times are simulated.
256 devices in a mesh: depth: 16 (over z_hi, x), height: 2 (over z_lo), batch: 8 (over y, core).
Axes of the slice: x: 4, y: 4, z: 8 (z_hi: 4, z_lo: 2; z = z_hi * 2 + z_lo), core: 2. Of those that a mesh axis runs over, the one named last changes fastest.
Arguments:
- volume: bfloat16 [8, 224, 28, 14, 384], P('batch', 'depth', 'height'), may hold values from -6 to 6
- patch_mask: int32 [8, 224, 28, 14], P('batch', 'depth', 'height'), may hold values 0 or 1
- mask_token: bfloat16 [384], replicated, may hold values from -4 to 4
- labels: int32 [8, 224, 28, 14], P('batch', 'depth', 'height'), may hold values from 0 to 3
- norm_gain: float32 [384], replicated, may hold values from 0.1 to 1.9
- qkv_weight: bfloat16 [384, 576], replicated, may hold values from -2 to 2
- proj_weight: bfloat16 [192, 384], replicated, may hold values from -0.4375 to 0.4375
- merge_gain: float32 [3072], replicated, may hold values from 0.1 to 1.9
- merge_weight: bfloat16 [3072, 768], P(None, 'height'), may hold values from -0.109375 to 0.109375
- upstream: bfloat16 [8, 224, 28, 14, 384], P('batch', 'depth', 'height'), may hold values from -6 to 6
Outputs:
- merged: bfloat16 [8, 112, 14, 7, 768], P('batch', 'depth', None, None, 'height')
- grad_qkv: float32 [384, 576], P(('depth', 'height'))
- grad_proj: float32 [192, 384], P(('depth', 'height'))
All inputs are finite; a program needn't handle non-finite values. No bound on the sum of `patch_mask` on one device may be relied on, other than what follows from the above.
Results may differ from a plain program's by a relative error of at most 0.034.
The roundings to bfloat16 on the way count: a program that leaves them out, or rounds other values in their place, can miss the bound.
Values may be sent and summed in bfloat16 or wider, within the bound.
A program may use at most 128 MiB of HBM per device.

v0:
```python
import functools
import math

import jax
import jax.numpy as jnp
import numpy as np
from jax import lax
from jax.experimental import pallas as pl
from jax.experimental.pallas import tpu as pltpu
from jax.sharding import PartitionSpec as P

HEADS = 6
HEAD = 32
ATTN = 192
C = 384
WIN = 7
SHIFT = 3
EDGE = 14
PITCH = 16
SLAB = EDGE * PITCH
ROWS = 384
FEED = C + ATTN
EPS = 1e-05
F32 = jnp.float32
BF16 = jnp.bfloat16
MESH = pl.DeviceIdType.MESH
VMEM_LIMIT = 56 * 2**20

SIZES = (3, 7, 4)
FIRST = (0, 3, 10)
ZONES = [(a, b) for a in range(3) for b in range(3)]


def up(value, unit):
    return -(-value // unit) * unit


ZONE_ROWS = {z: up(WIN * SIZES[z[0]] * SIZES[z[1]], 16) for z in ZONES}
ZONE_BASE = {}
TOTAL = 0
for zone in ZONES:
    ZONE_BASE[zone] = TOTAL
    TOTAL += ZONE_ROWS[zone]
PIECE_ROWS = tuple(up(WIN * s, 8) for s in SIZES)
PIECES = []
_at = 0
for _half in range(2):
    for _hz in range(3):
        PIECES.append((_half, _hz, _at))
        _at += PIECE_ROWS[_hz]

GROUPS = {
    (0, 0): ((1, 1),),
    (0, 1): ((1, 2), (1, 0)),
    (1, 0): ((2, 1), (0, 1)),
    (1, 1): ((2, 2), (2, 0), (0, 2), (0, 0)),
}


def slab_to_pieces():
    pick = np.zeros((SLAB, SLAB), np.float32)
    for half, hz, base in PIECES:
        for hh in range(SIZES[hz]):
            for k in range(WIN):
                width = (SHIFT + WIN * half + k) % EDGE
                pick[base + hh * WIN + k, (FIRST[hz] + hh) * PITCH + width] = 1
    return pick


def slab_to_cells():
    pick = np.zeros((SLAB, SLAB), np.float32)
    for hh in range(2):
        for ww in range(2):
            for h in range(7):
                for w in range(7):
                    pick[(hh * 2 + ww) * 56 + h * 8 + w, (2 * h + hh) * PITCH + 2 * w + ww] = 1
    return pick


def nn(a, b):
    return jnp.dot(a, b, preferred_element_type=F32)


def nt(a, b):
    return lax.dot_general(a, b, (((1,), (1,)), ((), ())), preferred_element_type=F32)


def tn(a, b):
    return lax.dot_general(a, b, (((0,), (0,)), ((), ())), preferred_element_type=F32)


def masked_pick(pick, mask_row):
    hidden = pick * mask_row
    return pick - hidden, jnp.sum(hidden.astype(F32), axis=1, keepdims=True)


AHEAD = {}
for _group, _members in GROUPS.items():
    _row = 0
    for zone in _members:
        if 0 in zone:
            AHEAD[zone] = (_group, _row)
        _row += ZONE_ROWS[zone]
HALO = list(AHEAD)
GROUP_LIST = list(GROUPS)


def neighbour(zone, by, sizes):
    device = {}
    for axis, part, size in zip(("depth", "height"), zone, sizes):
        if part == 0:
            device[axis] = lax.rem(lax.axis_index(axis) + by + size, size)
    return device


def front_kernel(sizes, vol, ups, mask, label, pick, token, gain, back_proj, weight, weight_t, eye, *rest):
    context_out, grad, x, space, pad_v, pad_u = rest[:6]
    send_buffers, rest = dict(zip(HALO, rest[6:11])), rest[11:]
    context_w, context_z, bias, proj, proj_t, dcon_t, con_t, dproj_t = rest[:8]
    ahead_send, ahead_recv, back_send, back_recv = rest[8:]

    def ahead(zone):
        group, row = AHEAD[zone]
        slot = HALO.index(zone)
        return pltpu.make_async_remote_copy(
            src_ref=send_buffers[zone],
            dst_ref=x.at[pl.ds(2 * GROUP_LIST.index(group), 2), pl.ds(row, ZONE_ROWS[zone]), :],
            send_sem=ahead_send.at[slot],
            recv_sem=ahead_recv.at[slot],
            device_id=neighbour(zone, -1, sizes),
            device_id_type=MESH,
        )

    def back(zone, half):
        group, row = AHEAD[zone]
        slot = 2 * HALO.index(zone) + half
        return pltpu.make_async_remote_copy(
            src_ref=context_w.at[2 * GROUP_LIST.index(group) + half, pl.ds(row, ZONE_ROWS[zone]), :],
            dst_ref=context_z.at[half, pl.ds(ZONE_BASE[zone], ZONE_ROWS[zone]), :],
            send_sem=back_send.at[slot],
            recv_sem=back_recv.at[slot],
            device_id=neighbour(zone, 1, sizes),
            device_id_type=MESH,
        )

    barrier = pltpu.get_barrier_semaphore()
    met = [((0, 1), -1), ((0, 1), 1), ((1, 0), 1), ((0, 0), -1), ((0, 0), 1)]
    for zone, by in met:
        pl.semaphore_signal(barrier, inc=1, device_id=neighbour(zone, by, sizes), device_id_type=MESH)

    space[...] = jnp.zeros_like(space)
    pad_v[...] = jnp.zeros_like(pad_v)
    pad_u[...] = jnp.zeros_like(pad_u)
    for number, group in enumerate(GROUP_LIST):
        used = sum(ZONE_ROWS[zone] for zone in GROUPS[group])
        x[2 * number : 2 * number + 2, used:, :] = jnp.zeros((2, ROWS - used, FEED), BF16)
    for d in range(EDGE):
        dz = 0 if d < FIRST[1] else 1 if d < FIRST[2] else 2
        at = d - FIRST[dz]
        for h in range(EDGE):
            pad_v[d % 2, h, 0:EDGE, :] = vol[0, d, h]
            pad_u[d % 2, h, 0:EDGE, :] = ups[0, d, h]
        shown, hidden = masked_pick(pick[...], mask[d])
        tokens = nn(shown, pad_v[d % 2].reshape(SLAB, C)) + hidden * token[...]
        mean = jnp.mean(tokens, axis=1, keepdims=True)
        centered = tokens - mean
        variance = jnp.mean(centered * centered, axis=1, keepdims=True)
        normed = centered * lax.rsqrt(variance + EPS) * gain[...]
        dcontext = nn(nn(pick[...], pad_u[d % 2].reshape(SLAB, C)).astype(BF16), back_proj[...])
        for half, hz, base in PIECES:
            size = WIN * SIZES[hz]
            row = ZONE_BASE[(dz, hz)] + at * size
            space[half, row : row + size, 0:C] = normed[base : base + size]
            space[half, row : row + size, C:FEED] = dcontext[base : base + size]
        if at == SIZES[dz] - 1:
            if dz == 0:
                pl.semaphore_wait(barrier, len(met))
            for hz in range(3):
                zone = (dz, hz)
                base, rows = ZONE_BASE[zone], ZONE_ROWS[zone]
                filled = space[:, base : base + rows, :].astype(BF16)
                if zone in AHEAD:
                    send_buffers[zone][...] = filled
                    ahead(zone).start()
                else:
                    group = GROUP_LIST.index(((dz - 1), (hz - 1)))
                    x[2 * group : 2 * group + 2, 0:rows, :] = filled

    grad[...] = jnp.zeros_like(grad)
    scale = HEAD**-0.5

    @pl.loop(0, 8)
    def _(i):
        for number, group in enumerate(GROUP_LIST):
            if number:

                @pl.when(i == 2 * number)
                def _():
                    for zone in GROUPS[group]:
                        if zone in AHEAD:
                            ahead(zone).wait_recv()

        normed = x[i, :, 0:C]
        label_row = label[i]
        label_column = jnp.transpose(jnp.broadcast_to(label_row, (8, ROWS)))[:, 0:1]
        bias[...] = jnp.where(label_column == label_row, 0.0, -1e30)
        proj[...] = nn(normed, weight[...]).astype(BF16)
        proj_t[...] = nt(weight_t[...], normed).astype(BF16)
        dcon_t[...] = nt(eye[...], x[i, :, C:FEED]).astype(BF16)
        for head in range(HEADS):
            a, b, c = (slice(k * ATTN + head * HEAD, k * ATTN + head * HEAD + HEAD) for k in range(3))
            scores = nn(proj[:, b], proj_t[a, :]) * (scale * math.log2(math.e)) + bias[...]
            exponent = jnp.exp2(scores - jnp.max(scores, axis=0, keepdims=True))
            weights = (exponent * (1.0 / jnp.sum(exponent, axis=0, keepdims=True))).astype(BF16)
            context_t = nn(proj_t[c, :], weights)
            con_t[a, :] = context_t
            inner = jnp.sum(dcon_t[a, :].astype(F32) * context_t, axis=0, keepdims=True)
            dweights = nn(proj[:, c], dcon_t[a, :])
            dscores = (weights.astype(F32) * (dweights - inner) * scale).astype(BF16)
            dproj_t[a, :] = nn(proj_t[b, :], dscores).astype(BF16)
            dproj_t[b, :] = jnp.transpose(nn(dscores, proj[:, a])).astype(BF16)
            cot = x[i, :, C + head * HEAD : C + head * HEAD + HEAD]
            dproj_t[c, :] = jnp.transpose(nn(weights, cot)).astype(BF16)
        context_w[i] = jnp.transpose(con_t[...]).astype(BF16)
        grad[...] += nn(dproj_t[...], normed)
        for number, group in enumerate(GROUP_LIST):
            if number:
                for half in range(2):

                    @pl.when(i == 2 * number + half)
                    def _():
                        for zone in GROUPS[group]:
                            if zone in AHEAD:
                                back(zone, half).start()

    for zone in HALO:
        ahead(zone).wait_send()
    for zone in ZONES:
        if zone not in AHEAD:
            group = GROUP_LIST.index((zone[0] - 1, zone[1] - 1))
            base, rows = ZONE_BASE[zone], ZONE_ROWS[zone]
            context_z[:, base : base + rows, :] = context_w[2 * group : 2 * group + 2, 0:rows, :]
    for zone in HALO:
        for half in range(2):
            back(zone, half).wait_recv()
    context_out[...] = context_z[...]
    for zone in HALO:
        for half in range(2):
            back(zone, half).wait_send()


def front(volume, upstream, mask, label, pick, token, gain, back_proj, weight, weight_t, eye, sizes):
    vmem = pl.BlockSpec(memory_space=pltpu.VMEM)
    operands = (volume, upstream, mask, label, pick, token, gain, back_proj, weight, weight_t, eye)
    return pl.pallas_call(
        functools.partial(front_kernel, sizes),
        out_shape=[
            jax.ShapeDtypeStruct((2, TOTAL, ATTN), BF16),
            jax.ShapeDtypeStruct((3 * ATTN, C), F32),
        ],
        in_specs=[vmem] * len(operands),
        out_specs=[vmem] * 2,
        scratch_shapes=[
            pltpu.VMEM((8, ROWS, FEED), BF16),
            pltpu.VMEM((2, TOTAL, FEED), F32),
            pltpu.VMEM((2, EDGE, PITCH, C), BF16),
            pltpu.VMEM((2, EDGE, PITCH, C), BF16),
        ]
        + [pltpu.VMEM((2, ZONE_ROWS[zone], FEED), BF16) for zone in HALO]
        + [
            pltpu.VMEM((8, ROWS, ATTN), BF16),
            pltpu.VMEM((2, TOTAL, ATTN), BF16),
            pltpu.VMEM((ROWS, ROWS), F32),
            pltpu.VMEM((ROWS, 3 * ATTN), BF16),
            pltpu.VMEM((3 * ATTN, ROWS), BF16),
            pltpu.VMEM((ATTN, ROWS), BF16),
            pltpu.VMEM((ATTN, ROWS), F32),
            pltpu.VMEM((3 * ATTN, ROWS), BF16),
            pltpu.SemaphoreType.DMA((5,)),
            pltpu.SemaphoreType.DMA((5,)),
            pltpu.SemaphoreType.DMA((10,)),
            pltpu.SemaphoreType.DMA((10,)),
        ],
        cost_estimate=pl.CostEstimate(flops=60_000_000_000, bytes_accessed=8_000_000, transcendentals=8_000_000),
        compiler_params=pltpu.CompilerParams(
            collective_id=1, has_side_effects=True, vmem_limit_bytes=VMEM_LIMIT
        ),
        name="front",
    )(*operands)


def merge_kernel(vol, ups, mask, pick, back, cells, token, proj, gain, own, other, *rest):
    contexts, own_out, other_out, grad_out, space, pad_v, pad_u, context_all, features = rest
    space[:, TOTAL:, :] = jnp.zeros((2, space.shape[1] - TOTAL, ATTN), F32)
    space[:, 0:TOTAL, :] = contexts[...].astype(F32)
    pad_v[...] = jnp.zeros_like(pad_v)
    pad_u[...] = jnp.zeros_like(pad_u)
    for pair in range(EDGE // 2):
        blocks = []
        for d in (2 * pair, 2 * pair + 1):
            dz = 0 if d < FIRST[1] else 1 if d < FIRST[2] else 2
            at = d - FIRST[dz]
            for h in range(EDGE):
                pad_v[d % 2, h, 0:EDGE, :] = vol[0, d, h]
                pad_u[d, h, 0:EDGE, :] = ups[0, d, h]
            pieces = []
            for half, hz, _ in PIECES:
                row = ZONE_BASE[(dz, hz)] + at * WIN * SIZES[hz]
                pieces.append(space[half, row : row + PIECE_ROWS[hz], :])
            context = nn(back[...], jnp.concatenate(pieces, axis=0).astype(BF16)).astype(BF16)
            context_all[d * SLAB : (d + 1) * SLAB, :] = context
            attended = nn(context, proj[...]).astype(BF16)
            shown, hidden = masked_pick(cells[...], mask[d])
            tokens = nn(shown, pad_v[d % 2].reshape(SLAB, C)) + hidden * token[...]
            block = (tokens + nn(cells[...], attended)).astype(BF16).astype(F32)
            blocks += [block[o * 56 : o * 56 + 56] for o in range(4)]
        total = sum(blocks[1:], blocks[0])
        mean = jnp.sum(total, axis=1, keepdims=True) * (1.0 / (8 * C))
        centered = [b - mean for b in blocks]
        squares = [b * b for b in centered]
        variance = jnp.sum(sum(squares[1:], squares[0]), axis=1, keepdims=True) * (1.0 / (8 * C))
        factor = lax.rsqrt(variance + EPS)
        for o in range(8):
            values = (centered[o] * factor * gain[o : o + 1, :]).astype(BF16)
            features[pair * 56 : pair * 56 + 56, o * C : (o + 1) * C] = values.astype(F32)
    merged = features[...].astype(BF16)
    own_out[...] = nn(merged, own[...]).astype(BF16)
    other_out[...] = nn(merged, other[...]).astype(BF16)
    grad_out[...] = tn(context_all[...], pad_u[...].reshape(EDGE * SLAB, C))


def merge(volume, upstream, mask, pick, back, cells, token, proj, gain, own, other, contexts):
    cells_out = jax.ShapeDtypeStruct((7 * 56, C), BF16)
    return pl.pallas_call(
        merge_kernel,
        out_shape=[cells_out, cells_out, jax.ShapeDtypeStruct((ATTN, C), F32)],
        scratch_shapes=[
            pltpu.VMEM((2, TOTAL + 32, ATTN), F32),
            pltpu.VMEM((2, EDGE, PITCH, C), BF16),
            pltpu.VMEM((EDGE, EDGE, PITCH, C), BF16),
            pltpu.VMEM((EDGE * SLAB, ATTN), BF16),
            pltpu.VMEM((7 * 56, 8 * C), F32),
        ],
        compiler_params=pltpu.CompilerParams(vmem_limit_bytes=VMEM_LIMIT),
        name="merge",
    )(volume, upstream, mask, pick, back, cells, token, proj, gain, own, other, contexts)


def reduce_kernel(sizes, terms, out, arrived, summed, gathered, send_a, recv_a, send_b, recv_b):
    depths, heights, batches = sizes
    owners = depths * heights
    depth, height, batch = (lax.axis_index(n) for n in ("depth", "height", "batch"))
    me = depth * heights + height

    def owner_at(step):
        other = lax.rem(me + step, owners)
        return {"depth": other // heights, "height": lax.rem(other, heights)}

    def batch_at(step):
        return {"batch": lax.rem(batch + step, batches)}

    barrier = pltpu.get_barrier_semaphore()

    @pl.loop(1, owners)
    def _(step):
        pl.semaphore_signal(barrier, inc=1, device_id=owner_at(step), device_id_type=MESH)

    @pl.loop(1, batches)
    def _(step):
        pl.semaphore_signal(barrier, inc=1, device_id=batch_at(step), device_id_type=MESH)

    pl.semaphore_wait(barrier, owners + batches - 2)

    def to_owner(step):
        return pltpu.make_async_remote_copy(
            src_ref=terms.at[lax.rem(me + step, owners)],
            dst_ref=arrived.at[step],
            send_sem=send_a.at[step],
            recv_sem=recv_a.at[step],
            device_id=owner_at(step),
            device_id_type=MESH,
        )

    @pl.loop(1, owners)
    def _(step):
        to_owner(step).start()

    summed[...] = terms[me].astype(F32)

    @pl.loop(1, owners)
    def _(step):
        to_owner(step).wait_recv()
        summed[...] += arrived[step].astype(F32)

    def to_batch(step):
        return pltpu.make_async_remote_copy(
            src_ref=summed,
            dst_ref=gathered.at[step],
            send_sem=send_b.at[step],
            recv_sem=recv_b.at[step],
            device_id=batch_at(step),
            device_id_type=MESH,
        )

    @pl.loop(1, batches)
    def _(step):
        to_batch(step).start()

    out[...] = summed[...]

    @pl.loop(1, batches)
    def _(step):
        to_batch(step).wait_recv()
        out[...] += gathered[step]

    @pl.loop(1, owners)
    def _(step):
        to_owner(step).wait_send()

    @pl.loop(1, batches)
    def _(step):
        to_batch(step).wait_send()


def reduce_terms(terms, sizes):
    owners, (rows, columns) = sizes[0] * sizes[1], terms.shape[1:]
    vmem = pl.BlockSpec(memory_space=pltpu.VMEM)
    return pl.pallas_call(
        functools.partial(reduce_kernel, sizes),
        out_shape=jax.ShapeDtypeStruct((rows, columns), F32),
        in_specs=[vmem],
        out_specs=vmem,
        scratch_shapes=[
            pltpu.VMEM((owners, rows, columns), terms.dtype),
            pltpu.VMEM((rows, columns), F32),
            pltpu.VMEM((sizes[2], rows, columns), F32),
            pltpu.SemaphoreType.DMA((owners,)),
            pltpu.SemaphoreType.DMA((owners,)),
            pltpu.SemaphoreType.DMA((sizes[2],)),
            pltpu.SemaphoreType.DMA((sizes[2],)),
        ],
        compiler_params=pltpu.CompilerParams(
            collective_id=0, has_side_effects=True, vmem_limit_bytes=VMEM_LIMIT
        ),
        name="reduce",
    )(terms)


def shifted(array, axes, by):
    sizes = [lax.axis_size(a) for a in axes]
    pairs = []
    for source in np.ndindex(*sizes):
        target = [(s + by) % n for s, n in zip(source, sizes)]
        pairs.append((int(np.ravel_multi_index(source, sizes)), int(np.ravel_multi_index(target, sizes))))
    return lax.ppermute(array, axes if len(axes) > 1 else axes[0], pairs)


def group_labels(labels, group):
    parts = []
    for zone in GROUPS[group]:
        spans = []
        for z in zone:
            start = {1: 0, 2: WIN, 0: WIN + SIZES[2]}[z]
            spans.append((start, SIZES[z]))
        (d, nd), (h, nh) = spans
        part = labels[d : d + nd, h : h + nh].reshape(nd, nh, 2, WIN).transpose(2, 0, 1, 3)
        part = part.reshape(2, nd * nh * WIN)
        parts.append(jnp.pad(part, ((0, 0), (0, ZONE_ROWS[zone] - nd * nh * WIN)), constant_values=-1))
    row = jnp.concatenate(parts, axis=1)
    row = jnp.pad(row, ((0, 0), (0, ROWS - row.shape[1])), constant_values=-1)
    return row.reshape(2, 1, ROWS).astype(F32)


def shards(
    volume,
    patch_mask,
    mask_token,
    labels,
    norm_gain,
    qkv_weight,
    proj_weight,
    merge_gain,
    merge_weight,
    upstream,
):
    sizes = tuple(lax.axis_size(n) for n in ("depth", "height", "batch"))
    height, batch = lax.axis_index("height"), lax.axis_index("batch")
    pick_np = slab_to_pieces()
    pick = jnp.asarray(pick_np, BF16)
    back = jnp.asarray(pick_np.T, BF16)
    cells = jnp.asarray(slab_to_cells(), BF16)
    eye = jnp.asarray(np.eye(ATTN), BF16)
    token = mask_token.reshape(1, C).astype(F32)
    mask = jnp.pad(patch_mask[0], ((0, 0), (0, 0), (0, PITCH - EDGE))).reshape(EDGE, 1, SLAB).astype(BF16)
    label = jnp.concatenate([group_labels(labels[0], group) for group in GROUP_LIST], 0)
    contexts, total = front(
        volume,
        upstream,
        mask,
        label,
        pick,
        token,
        norm_gain.reshape(1, C),
        proj_weight.T,
        qkv_weight,
        qkv_weight.T,
        eye,
        sizes,
    )

    share = 8 * C // sizes[2]
    rows = lax.dynamic_slice_in_dim(merge_weight, batch * share, share, 0)
    other = lax.all_gather(shifted(rows, ("height",), 1), "batch", axis=0, tiled=True)

    own_part, other_part, grad_proj = merge(
        volume,
        upstream,
        mask,
        pick,
        back,
        cells,
        token,
        proj_weight,
        merge_gain.reshape(8, C),
        merge_weight,
        other,
        contexts,
    )
    fetched = shifted(other_part, ("height",), 1)
    owners = sizes[0] * sizes[1]
    terms = jnp.concatenate(
        (total.T.reshape(owners, -1, 3 * ATTN), grad_proj.reshape(owners, -1, 3 * ATTN)), 1
    ).astype(BF16)
    sums = reduce_terms(terms, sizes)
    lines = C // owners
    grad_qkv = sums[:lines]
    grad_proj = sums[lines:].reshape(ATTN // owners, C)

    halves = [part.reshape(7, 7, 8, C)[:, :, :7] for part in (own_part, fetched)]
    low = jnp.where(height == 0, halves[0], halves[1])
    high = jnp.where(height == 0, halves[1], halves[0])
    merged = jnp.concatenate((low, high), 1)[None]
    return (merged, grad_qkv, grad_proj)


def solution(mesh):
    return jax.shard_map(
        shards,
        mesh=mesh,
        in_specs=(
            P("batch", "depth", "height", None, None),
            P("batch", "depth", "height", None),
            P(),
            P("batch", "depth", "height", None),
            P(),
            P(),
            P(),
            P(),
            P(None, "height"),
            P("batch", "depth", "height", None, None),
        ),
        out_specs=(
            P("batch", "depth", None, None, "height"),
            P(("depth", "height"), None),
            P(("depth", "height"), None),
        ),
        check_vma=False,
    )
```

profile of v0, /device:TPU:1, one launch (start us, length us, event | category | flops | bytes accessed | tf_op | source)
XLA Modules:
  0.0 174.0 jit_solution(6478590364902376232)
XLA Ops:
  7.2 0.0 all-gather.2.cloned.1.call-start
  7.2 1.1 constant_dynamic-slice_fusion
  8.3 2.6 %collective-permute-start = (bf16[384,384]{1,0:T(8,128)(2,1)S(1)}, bf16[384,384]{1,0:T(8,128)(2,1)S(1)}, u32[]{:S(2)}, u32[]{:S(2)}) collective-permute-start(bf16[384,384]{1,0:T(8,128)(2,1)S(1)} %constant_dynamic-slice_fusion), channel_id=1, source_target_pairs={{0,8},{8,0},{1,9},{9,1},{2,10},{10,2},{3,11},{11,3},{4,12},{12,4},... | collective-permute-start | bytes 884744 | tf_op jit(solution)/shard_map/ppermute | solution.py:455
  10.9 0.9 copy.55
  11.9 1.3 reshape.133.token
  13.1 1.2 reshape.127.gain
  14.4 1.3 reshape.108.gain
  15.7 1.0 convert.15
  16.7 0.7 convert_element_type.45.mask
  17.4 0.1 reshape.125
  17.5 0.1 reshape.126
  17.6 0.1 reshape.123
  17.7 0.1 reshape.124
  17.8 0.1 reshape.121
  17.9 0.1 reshape.122
  18.0 0.1 reshape.119
  18.1 0.1 reshape.120
  18.2 0.1 fusion.2
  18.3 0.1 reshape.117
  18.4 0.1 reshape.118
  18.5 0.1 reshape.113
  18.6 0.1 reshape.114
  18.7 0.1 reshape.111
  18.8 0.1 reshape.112
  18.9 0.1 select_add_fusion.1
  19.0 0.1 reshape.115
  19.1 0.1 reshape.116
  19.2 0.1 select_add_fusion
  19.3 0.1 reshape.109
  19.4 0.1 reshape.110
  19.6 0.8 copy.41
  20.4 1.0 copy.43.weight
  21.4 0.6 pad_maximum_fusion.1.label
  22.0 0.7 copy-done.4
  22.8 91.8 %front.1 = (bf16[2,1456,192]{2,1,0:T(8,128)(2,1)}, f32[576,384]{1,0:T(8,128)}) custom-call(bf16[1,14,14,14,384]{4,3,2,1,0:T(8,128)(2,1)} %vol.3, bf16[1,14,14,14,384]{4,3,2,1,0:T(8,128)(2,1)} %ups.3, bf16[14,1,224]{2,1,0:T(2,128)(2,1)} %convert_element_type.45.mask, f32[8,1,384]{2,1,0:T(1,128)} %pad_maximum_fusion.1.label, ...), custom_call_target="tpu_custom_call" | custom-call | flops 60000002048 | bytes 8000000 | tf_op jit(solution)/shard_map/front/pallas_call | solution.py:255
  114.6 14.7 %merge.1 = (bf16[392,384]{1,0:T(8,128)(2,1)}, bf16[392,384]{1,0:T(8,128)(2,1)}, f32[192,384]{1,0:T(8,128)}) custom-call(bf16[1,14,14,14,384]{4,3,2,1,0:T(8,128)(2,1)} %vol.3, bf16[1,14,14,14,384]{4,3,2,1,0:T(8,128)(2,1)} %ups.3, bf16[14,1,224]{2,1,0:T(2,128)(2,1)} %convert_element_type.45.mask, bf16[224,224]{1,0:T(8,128)(2,1)} %constant.27.clone.pick, ...), custom_call_target="tpu_custom_call" | custom-call | tf_op jit(solution)/shard_map/merge/pallas_call | solution.py:334
  129.3 1.6 collective-permute-start.1
  130.9 0.1 convert_bitcast_fusion
  130.9 0.3 copy.45
  131.2 0.1 reshape.130
  131.4 0.2 reshape.131
  131.6 1.0 pad_maximum_fusion.terms
  132.6 31.3 %reduce.1 = f32[16,576]{1,0:T(8,128)} custom-call(bf16[32,16,576]{2,1,0:T(8,128)(2,1)} %pad_maximum_fusion.terms), custom_call_target="tpu_custom_call" | custom-call | tf_op jit(solution)/shard_map/reduce/pallas_call | solution.py:428
  164.0 0.8 slice.51
  164.8 0.7 reshape.132
  165.4 0.1 broadcast_select_fusion.1
  165.5 1.0 maximum_bitcast_fusion
  166.5 0.6 copy.63
  (49 shorter events, 0.3 us)
Async XLA Ops:
  7.2 12.4 %copy-start.1 = (bf16[192,384]{1,0:T(8,128)(2,1)S(1)}, bf16[192,384]{1,0:T(8,128)(2,1)}, u32[]{:S(2)}) copy-start(bf16[192,384]{1,0:T(8,128)(2,1)} %proj.1) | copy-start | bytes 442372
  7.2 13.2 %copy-start.2 = (bf16[384,576]{0,1:T(8,128)(2,1)S(1)}, bf16[384,576]{0,1:T(8,128)(2,1)}, u32[]{:S(2)}) copy-start(bf16[384,576]{0,1:T(8,128)(2,1)} %param.19) | copy-start | bytes 1327108
  7.2 107.4 %all-gather.2.cloned.1.call-start = ((), (), s32[]{:S(2)}) async-start(), calls=%async_computation | async-start | bytes 2654208 | tf_op jit(solution)/shard_map/all_gather | solution.py:513
  8.3 13.7 %collective-permute-start = (bf16[384,384]{1,0:T(8,128)(2,1)S(1)}, bf16[384,384]{1,0:T(8,128)(2,1)S(1)}, u32[]{:S(2)}, u32[]{:S(2)}) collective-permute-start(bf16[384,384]{1,0:T(8,128)(2,1)S(1)} %constant_dynamic-slice_fusion), channel_id=1, source_target_pairs={{0,8},{8,0},{1,9},{9,1},{2,10},{10,2},{3,11},{11,3},{4,12},{12,4},... | collective-permute-start | bytes 884744 | tf_op jit(solution)/shard_map/ppermute | solution.py:455
  22.0 0.7 copy-start.4
  114.6 16.3 %copy-start = (f32[576,384]{1,0:T(8,128)S(1)}, f32[576,384]{1,0:T(8,128)}, u32[]{:S(2)}) copy-start(f32[576,384]{1,0:T(8,128)} %get-tuple-element.11) | copy-start | bytes 2654212
  129.3 2.0 %copy-start.5 = (f32[192,384]{1,0:T(8,128)S(1)}, f32[192,384]{1,0:T(8,128)}, u32[]{:S(2)}) copy-start(f32[192,384]{1,0:T(8,128)} %get-tuple-element.12) | copy-start | bytes 884740
  129.3 36.1 %collective-permute-start.1 = (bf16[392,384]{1,0:T(8,128)(2,1)}, bf16[392,384]{1,0:T(8,128)(2,1)S(1)}, u32[]{:S(2)}, u32[]{:S(2)}) collective-permute-start(bf16[392,384]{1,0:T(8,128)(2,1)} %get-tuple-element.10), channel_id=1, source_target_pairs={{0,8},{8,0},{1,9},{9,1},{2,10},{10,2},{3,11},{11,3},{4,12},{12,4},... | collective-permute-start | bytes 903176 | tf_op jit(solution)/shard_map/ppermute | solution.py:455
  130.9 34.5 %copy-start.3 = (bf16[392,384]{1,0:T(8,128)(2,1)S(1)}, bf16[392,384]{1,0:T(8,128)(2,1)}, u32[]{:S(2)}) copy-start(bf16[392,384]{1,0:T(8,128)(2,1)} %get-tuple-element.9) | copy-start | bytes 903172
  163.9 2.5 %copy-start.6 = (f32[16,576]{1,0:T(8,128)S(1)}, f32[16,576]{1,0:T(8,128)}, u32[]{:S(2)}) copy-start(f32[16,576]{1,0:T(8,128)} %reduce.1) | copy-start | bytes 110596
Sparse Core Ops, SparseCore 0:
  22.9 30.9 all-gather.1
where the time goes:
time: 176 us; the launch traced here: 174 us
  Pallas kernels  138 us (78%)
  between operations  14.4 us (8%)
  local copies, waits for them, and re-layouts  13.6 us (8%)
  starting transfers between devices  4.14 us (2%)
  other arithmetic  3.98 us (2%)
    pallas_call x1, Pallas kernels, front(): pl.pallas_call(functools.partial(front_kernel, sizes), out_shape=[jax.Sha...  91.8 us
    pallas_call x1, Pallas kernels, reduce_terms(): pl.pallas_call(functools.partial(reduce_kernel, sizes), out_shape=jax.Sha...  31.3 us
    pallas_call x1, Pallas kernels, merge(): pl.pallas_call(merge_kernel, out_shape=[cells_out, cells_out, jax.ShapeDt...  14.7 us
    ppermute x2, starting transfers between devices, shifted(): return lax.ppermute(array, axes if len(axes) > 1 else axes[0], pairs)  4.1 us
    unnamed x19, local copies, waits for them, and re-layouts  4.1 us
  transfers between devices with their start and end apart: 3, of which 0 were waited for; matrix products, arithmetic and copies ran while one was open for 8% of the time, Pallas kernels for 71%

commit v1 on v0

v1 whole, which is shorter than its diff:
```python
import functools
import math

import jax
import jax.numpy as jnp
import numpy as np
from jax import lax
from jax.experimental import pallas as pl
from jax.experimental.pallas import tpu as pltpu
from jax.sharding import PartitionSpec as P

HEADS = 6
HEAD = 32
ATTN = 192
C = 384
WIN = 7
SHIFT = 3
EDGE = 14
PITCH = 16
SLAB = EDGE * PITCH
ROWS = 384
FEED = C + ATTN
EPS = 1e-05
F32 = jnp.float32
BF16 = jnp.bfloat16
MESH = pl.DeviceIdType.MESH
VMEM_LIMIT = 56 * 2**20

SIZES = (3, 7, 4)
FIRST = (0, 3, 10)
ZONES = [(a, b) for a in range(3) for b in range(3)]


def up(value, unit):
    return -(-value // unit) * unit


ZONE_ROWS = {z: up(WIN * SIZES[z[0]] * SIZES[z[1]], 16) for z in ZONES}
ZONE_BASE = {}
TOTAL = 0
for zone in ZONES:
    ZONE_BASE[zone] = TOTAL
    TOTAL += ZONE_ROWS[zone]
PIECE_ROWS = tuple(up(WIN * s, 8) for s in SIZES)
PIECES = []
_at = 0
for _half in range(2):
    for _hz in range(3):
        PIECES.append((_half, _hz, _at))
        _at += PIECE_ROWS[_hz]

GROUPS = {
    (0, 0): ((1, 1),),
    (0, 1): ((1, 2), (1, 0)),
    (1, 0): ((2, 1), (0, 1)),
    (1, 1): ((2, 2), (2, 0), (0, 2), (0, 0)),
}


def slab_to_pieces():
    pick = np.zeros((SLAB, SLAB), np.float32)
    for half, hz, base in PIECES:
        for hh in range(SIZES[hz]):
            for k in range(WIN):
                width = (SHIFT + WIN * half + k) % EDGE
                pick[base + hh * WIN + k, (FIRST[hz] + hh) * PITCH + width] = 1
    return pick


def slab_to_cells():
    pick = np.zeros((SLAB, SLAB), np.float32)
    for hh in range(2):
        for ww in range(2):
            for h in range(7):
                for w in range(7):
                    pick[(hh * 2 + ww) * 56 + h * 8 + w, (2 * h + hh) * PITCH + 2 * w + ww] = 1
    return pick


def nn(a, b):
    return jnp.dot(a, b, preferred_element_type=F32)


def nt(a, b):
    return lax.dot_general(a, b, (((1,), (1,)), ((), ())), preferred_element_type=F32)


def tn(a, b):
    return lax.dot_general(a, b, (((0,), (0,)), ((), ())), preferred_element_type=F32)


def masked_pick(pick, mask_row):
    hidden = pick * mask_row
    return pick - hidden, jnp.sum(hidden.astype(F32), axis=1, keepdims=True)


AHEAD = {}
for _group, _members in GROUPS.items():
    _row = 0
    for zone in _members:
        if 0 in zone:
            AHEAD[zone] = (_group, _row)
        _row += ZONE_ROWS[zone]
HALO = list(AHEAD)
GROUP_LIST = list(GROUPS)


def neighbour(zone, by, sizes):
    device = {}
    for axis, part, size in zip(("depth", "height"), zone, sizes):
        if part == 0:
            device[axis] = lax.rem(lax.axis_index(axis) + by + size, size)
    return device


def zone_of(d):
    dz = 0 if d < FIRST[1] else 1 if d < FIRST[2] else 2
    return dz, d - FIRST[dz]


def block_kernel(sizes, *refs):
    depths, heights, batches = sizes
    owners = depths * heights
    lines = C // owners
    vol, ups, mask, label, pick, back_pick, cells, params, weight, weight_p, eye, own = refs[:12]
    merged_out, grad_qkv_out, grad_proj_out = refs[12:15]
    x, space, pad_v, pad_u, context_w, context_z, bias, proj, proj_t, dcon_t, con_t, dproj_t = refs[15:27]
    weight_t, grad, context_space, context_all, features, other, sent, fetched = refs[27:35]
    terms, arrived, total, gathered, ahead_send, ahead_recv, back_send, back_recv = refs[35:43]
    share_send, share_recv, merged_send, merged_recv = refs[43:47]
    term_send, term_recv, sum_send, sum_recv = refs[47:51]
    send_buffers = dict(zip(HALO, refs[51:56]))

    depth, height, batch = (lax.axis_index(n) for n in ("depth", "height", "batch"))
    me = depth * heights + height
    peer = {"height": heights - 1 - height}

    def owner_at(step):
        to = lax.rem(me + step, owners)
        return {"depth": to // heights, "height": lax.rem(to, heights)}

    def batch_at(step):
        return {"batch": lax.rem(batch + step, batches)}

    def remote(src, dst, send, recv, device):
        return pltpu.make_async_remote_copy(
            src_ref=src, dst_ref=dst, send_sem=send, recv_sem=recv, device_id=device, device_id_type=MESH
        )

    def ahead(zone):
        group, row = AHEAD[zone]
        slot = HALO.index(zone)
        landing = x.at[pl.ds(2 * GROUP_LIST.index(group), 2), pl.ds(row, ZONE_ROWS[zone]), :]
        return remote(
            send_buffers[zone], landing, ahead_send.at[slot], ahead_recv.at[slot], neighbour(zone, -1, sizes)
        )

    def back(zone, half):
        group, row = AHEAD[zone]
        slot = 2 * HALO.index(zone) + half
        return remote(
            context_w.at[2 * GROUP_LIST.index(group) + half, pl.ds(row, ZONE_ROWS[zone]), :],
            context_z.at[half, pl.ds(ZONE_BASE[zone], ZONE_ROWS[zone]), :],
            back_send.at[slot],
            back_recv.at[slot],
            neighbour(zone, 1, sizes),
        )

    def first_share():
        return remote(own.at[batch], other.at[0], share_send.at[0], share_recv.at[0], peer)

    def next_share(step):
        return remote(other.at[0], other.at[step], share_send.at[step], share_recv.at[step], batch_at(step))

    def swap_merged():
        return remote(sent, fetched, merged_send.at[0], merged_recv.at[0], peer)

    def term(kind, step):
        return remote(
            terms[kind].at[lax.rem(me + step, owners)],
            arrived[kind].at[step],
            term_send.at[kind, step],
            term_recv.at[kind, step],
            owner_at(step),
        )

    def to_batch(step):
        return remote(total, gathered.at[step], sum_send.at[step], sum_recv.at[step], batch_at(step))

    barrier = pltpu.get_barrier_semaphore()

    @pl.loop(1, owners)
    def _(step):
        pl.semaphore_signal(barrier, inc=1, device_id=owner_at(step), device_id_type=MESH)

    @pl.loop(1, batches)
    def _(step):
        pl.semaphore_signal(barrier, inc=1, device_id=batch_at(step), device_id_type=MESH)

    gain, token = params[0:1, :], params[1:2, :]
    space[...] = jnp.zeros_like(space)
    pad_v[...] = jnp.zeros_like(pad_v)
    pad_u[...] = jnp.zeros_like(pad_u)
    for number, group in enumerate(GROUP_LIST):
        used = sum(ZONE_ROWS[zone] for zone in GROUPS[group])
        x[2 * number : 2 * number + 2, used:, :] = jnp.zeros((2, ROWS - used, FEED), BF16)
    for d in range(EDGE):
        dz, at = zone_of(d)
        for h in range(EDGE):
            pad_v[d % 2, h, 0:EDGE, :] = vol[0, d, h]
            pad_u[d, h, 0:EDGE, :] = ups[0, d, h]
        shown, hidden = masked_pick(pick[...], mask[d])
        tokens = nn(shown, pad_v[d % 2].reshape(SLAB, C)) + hidden * token
        mean = jnp.mean(tokens, axis=1, keepdims=True)
        centered = tokens - mean
        variance = jnp.mean(centered * centered, axis=1, keepdims=True)
        normed = centered * lax.rsqrt(variance + EPS) * gain
        dcontext = nt(nn(pick[...], pad_u[d].reshape(SLAB, C)).astype(BF16), weight_p[...])
        for half, hz, base in PIECES:
            size = WIN * SIZES[hz]
            row = ZONE_BASE[(dz, hz)] + at * size
            space[half, row : row + size, 0:C] = normed[base : base + size]
            space[half, row : row + size, C:FEED] = dcontext[base : base + size]
        if at == SIZES[dz] - 1:
            if dz == 0:
                pl.semaphore_wait(barrier, owners + batches - 2)
            for hz in range(3):
                zone = (dz, hz)
                base, rows = ZONE_BASE[zone], ZONE_ROWS[zone]
                filled = space[:, base : base + rows, :].astype(BF16)
                if zone in AHEAD:
                    send_buffers[zone][...] = filled
                    ahead(zone).start()
                else:
                    group = GROUP_LIST.index(((dz - 1), (hz - 1)))
                    x[2 * group : 2 * group + 2, 0:rows, :] = filled
    first_share().start()

    weight_t[...] = jnp.transpose(weight[...].astype(F32)).astype(BF16)
    grad[...] = jnp.zeros_like(grad)
    scale = HEAD**-0.5
    late = 1 - (lax.rem(depth, 4) + 3) // 4

    @pl.loop(0, 8)
    def _(turn):
        pair = turn // 2
        i = turn + late * pair * (3 - pair) * (3 - 2 * pair)
        for number, group in enumerate(GROUP_LIST):
            if number:

                @pl.when(i == 2 * number)
                def _():
                    for zone in GROUPS[group]:
                        if zone in AHEAD:
                            ahead(zone).wait_recv()

        @pl.when(turn == 3)
        def _():
            first_share().wait_recv()

            @pl.loop(1, batches)
            def _(step):
                next_share(step).start()

        normed = x[i, :, 0:C]
        label_row = label[i]
        label_column = jnp.transpose(jnp.broadcast_to(label_row, (8, ROWS)))[:, 0:1]
        bias[...] = jnp.where(label_column == label_row, 0.0, -1e30)
        proj[...] = nn(normed, weight[...]).astype(BF16)
        proj_t[...] = nt(weight_t[...], normed).astype(BF16)
        dcon_t[...] = nt(eye[...], x[i, :, C:FEED]).astype(BF16)
        for head in range(HEADS):
            a, b, c = (slice(k * ATTN + head * HEAD, k * ATTN + head * HEAD + HEAD) for k in range(3))
            scores = nn(proj[:, b], proj_t[a, :]) * (scale * math.log2(math.e)) + bias[...]
            exponent = jnp.exp2(scores - jnp.max(scores, axis=0, keepdims=True))
            weights = (exponent * (1.0 / jnp.sum(exponent, axis=0, keepdims=True))).astype(BF16)
            context_t = nn(proj_t[c, :], weights)
            con_t[a, :] = context_t
            inner = jnp.sum(dcon_t[a, :].astype(F32) * context_t, axis=0, keepdims=True)
            dweights = nn(proj[:, c], dcon_t[a, :])
            dscores = (weights.astype(F32) * (dweights - inner) * scale).astype(BF16)
            dproj_t[a, :] = nn(proj_t[b, :], dscores).astype(BF16)
            dproj_t[b, :] = jnp.transpose(nn(dscores, proj[:, a])).astype(BF16)
            cot = x[i, :, C + head * HEAD : C + head * HEAD + HEAD]
            dproj_t[c, :] = jnp.transpose(nn(weights, cot)).astype(BF16)
        context_w[i] = jnp.transpose(con_t[...]).astype(BF16)
        grad[...] += nn(dproj_t[...], normed)
        for number, group in enumerate(GROUP_LIST):
            if number:
                for half in range(2):

                    @pl.when(i == 2 * number + half)
                    def _():
                        for zone in GROUPS[group]:
                            if zone in AHEAD:
                                back(zone, half).start()

    spread = jnp.transpose(grad[...])
    terms[0][...] = jnp.zeros_like(terms[0])
    for o in range(owners):
        terms[0][o, 0:lines, 0 : 3 * ATTN] = spread[o * lines : (o + 1) * lines].astype(BF16)

    @pl.loop(1, owners)
    def _(step):
        term(0, step).start()

    for zone in ZONES:
        if zone not in AHEAD:
            group = GROUP_LIST.index((zone[0] - 1, zone[1] - 1))
            base, rows = ZONE_BASE[zone], ZONE_ROWS[zone]
            context_z[:, base : base + rows, :] = context_w[2 * group : 2 * group + 2, 0:rows, :]
    for zone in HALO:
        for half in range(2):
            back(zone, half).wait_recv()
    context_space[:, TOTAL:, :] = jnp.zeros((2, context_space.shape[1] - TOTAL, ATTN), F32)
    context_space[:, 0:TOTAL, :] = context_z[...].astype(F32)
    for pair in range(EDGE // 2):
        blocks = []
        for d in (2 * pair, 2 * pair + 1):
            dz, at = zone_of(d)
            for h in range(EDGE):
                pad_v[d % 2, h, 0:EDGE, :] = vol[0, d, h]
            pieces = []
            for half, hz, _ in PIECES:
                row = ZONE_BASE[(dz, hz)] + at * WIN * SIZES[hz]
                pieces.append(context_space[half, row : row + PIECE_ROWS[hz], :])
            context = nn(back_pick[...], jnp.concatenate(pieces, axis=0).astype(BF16)).astype(BF16)
            context_all[d * SLAB : (d + 1) * SLAB, :] = context
            attended = nn(context, weight_p[...]).astype(BF16)
            shown, hidden = masked_pick(cells[...], mask[d])
            tokens = nn(shown, pad_v[d % 2].reshape(SLAB, C)) + hidden * token
            block = (tokens + nn(cells[...], attended)).astype(BF16).astype(F32)
            blocks += [block[o * 56 : o * 56 + 56] for o in range(4)]
        summed = sum(blocks[1:], blocks[0])
        mean = jnp.sum(summed, axis=1, keepdims=True) * (1.0 / (8 * C))
        centered = [b - mean for b in blocks]
        squares = [b * b for b in centered]
        variance = jnp.sum(sum(squares[1:], squares[0]), axis=1, keepdims=True) * (1.0 / (8 * C))
        factor = lax.rsqrt(variance + EPS)
        for o in range(8):
            features[o, pair * 56 : pair * 56 + 56, :] = centered[o] * factor * params[2 + o : 3 + o, :]

    grad_proj = tn(context_all[...], pad_u[...].reshape(EDGE * SLAB, C))
    terms[1][...] = jnp.zeros_like(terms[1])
    per = ATTN // owners
    for o in range(owners):
        rows = grad_proj[o * per : (o + 1) * per].astype(BF16)
        terms[1][o, 0:per, 0:ATTN] = rows[:, 0:ATTN]
        terms[1][o, per : 2 * per, 0:ATTN] = rows[:, ATTN:]

    @pl.loop(1, owners)
    def _(step):
        term(1, step).start()

    @pl.loop(1, batches)
    def _(step):
        next_share(step).wait_recv()

    each = 8 // batches
    result = jnp.zeros(features.shape[1:], F32)
    for step in range(batches):
        at = lax.rem(batch - step + batches, batches) * each
        for k in range(each):
            result += nn(features[at + k].astype(BF16), other[step, k * C : (k + 1) * C, :])
    sent[0 : result.shape[0], :] = result.astype(BF16)
    sent[result.shape[0] :, :] = jnp.zeros((sent.shape[0] - result.shape[0], C), BF16)
    swap_merged().start()
    result = jnp.zeros(features.shape[1:], F32)
    for step in range(batches):
        for k in range(each):
            result += nn(features[step * each + k].astype(BF16), own[step, k * C : (k + 1) * C, :])
    merged_out[height] = result.astype(BF16)

    wide = terms[0].shape[2]
    total[:, 0:wide] = terms[0][me].astype(F32)
    total[:, wide:] = terms[1][me].astype(F32)

    @pl.loop(1, owners)
    def _(step):
        term(0, step).wait_recv()
        total[:, 0:wide] += arrived[0][step].astype(F32)

    @pl.loop(1, owners)
    def _(step):
        term(1, step).wait_recv()
        total[:, wide:] += arrived[1][step].astype(F32)

    @pl.loop(1, batches)
    def _(step):
        to_batch(step).start()

    swap_merged().wait_recv()
    merged_out[heights - 1 - height] = fetched[0 : result.shape[0], :]
    gathered[0] = total[...]

    @pl.loop(1, batches)
    def _(step):
        to_batch(step).wait_recv()
        gathered[0] += gathered[step]

    grad_qkv_out[...] = gathered[0, 0:lines, 0 : 3 * ATTN]
    grad_proj_out[:, 0:ATTN] = gathered[0, 0:per, wide : wide + ATTN]
    grad_proj_out[:, ATTN:] = gathered[0, per : 2 * per, wide : wide + ATTN]

    for zone in HALO:
        ahead(zone).wait_send()
        for half in range(2):
            back(zone, half).wait_send()
    first_share().wait_send()
    swap_merged().wait_send()

    @pl.loop(1, owners)
    def _(step):
        term(0, step).wait_send()
        term(1, step).wait_send()

    @pl.loop(1, batches)
    def _(step):
        next_share(step).wait_send()
        to_batch(step).wait_send()


def run_block(operands, sizes):
    vmem = pl.BlockSpec(memory_space=pltpu.VMEM)
    owners, batches = sizes[0] * sizes[1], sizes[2]
    lines = up(C // owners, 16)
    wide, narrow = up(3 * ATTN, 128), up(ATTN, 128)
    cell_rows = 7 * 56

    def pair_of(rows):
        return [pltpu.VMEM((rows, lines, wide), BF16), pltpu.VMEM((rows, lines, narrow), BF16)]

    return pl.pallas_call(
        functools.partial(block_kernel, sizes),
        out_shape=[
            jax.ShapeDtypeStruct((2, cell_rows, C), BF16),
            jax.ShapeDtypeStruct((C // owners, 3 * ATTN), F32),
            jax.ShapeDtypeStruct((ATTN // owners, C), F32),
        ],
        in_specs=[vmem] * len(operands),
        out_specs=[vmem] * 3,
        scratch_shapes=[
            pltpu.VMEM((8, ROWS, FEED), BF16),
            pltpu.VMEM((2, TOTAL, FEED), F32),
            pltpu.VMEM((2, EDGE, PITCH, C), BF16),
            pltpu.VMEM((EDGE, EDGE, PITCH, C), BF16),
            pltpu.VMEM((8, ROWS, ATTN), BF16),
            pltpu.VMEM((2, TOTAL, ATTN), BF16),
            pltpu.VMEM((ROWS, ROWS), F32),
            pltpu.VMEM((ROWS, 3 * ATTN), BF16),
            pltpu.VMEM((3 * ATTN, ROWS), BF16),
            pltpu.VMEM((ATTN, ROWS), BF16),
            pltpu.VMEM((ATTN, ROWS), F32),
            pltpu.VMEM((3 * ATTN, ROWS), BF16),
            pltpu.VMEM((3 * ATTN, C), BF16),
            pltpu.VMEM((3 * ATTN, C), F32),
            pltpu.VMEM((2, TOTAL + 32, ATTN), F32),
            pltpu.VMEM((EDGE * SLAB, ATTN), BF16),
            pltpu.VMEM((8, cell_rows, C), F32),
            pltpu.VMEM((batches, 8 * C // batches, C), BF16),
            pltpu.VMEM((up(cell_rows, 16), C), BF16),
            pltpu.VMEM((up(cell_rows, 16), C), BF16),
            pair_of(owners),
            pair_of(owners),
            pltpu.VMEM((lines, wide + narrow), F32),
            pltpu.VMEM((batches, lines, wide + narrow), F32),
            pltpu.SemaphoreType.DMA((5,)),
            pltpu.SemaphoreType.DMA((5,)),
            pltpu.SemaphoreType.DMA((10,)),
            pltpu.SemaphoreType.DMA((10,)),
            pltpu.SemaphoreType.DMA((batches,)),
            pltpu.SemaphoreType.DMA((batches,)),
            pltpu.SemaphoreType.DMA((1,)),
            pltpu.SemaphoreType.DMA((1,)),
            pltpu.SemaphoreType.DMA((2, owners)),
            pltpu.SemaphoreType.DMA((2, owners)),
            pltpu.SemaphoreType.DMA((batches,)),
            pltpu.SemaphoreType.DMA((batches,)),
        ]
        + [pltpu.VMEM((2, ZONE_ROWS[zone], FEED), BF16) for zone in HALO],
        cost_estimate=pl.CostEstimate(flops=80_000_000_000, bytes_accessed=12_000_000, transcendentals=8_000_000),
        compiler_params=pltpu.CompilerParams(
            collective_id=1, has_side_effects=True, vmem_limit_bytes=VMEM_LIMIT
        ),
        name="block",
    )(*operands)


def group_labels(labels, group):
    parts = []
    for zone in GROUPS[group]:
        spans = []
        for z in zone:
            start = {1: 0, 2: WIN, 0: WIN + SIZES[2]}[z]
            spans.append((start, SIZES[z]))
        (d, nd), (h, nh) = spans
        part = labels[d : d + nd, h : h + nh].reshape(nd, nh, 2, WIN).transpose(2, 0, 1, 3)
        part = part.reshape(2, nd * nh * WIN)
        parts.append(jnp.pad(part, ((0, 0), (0, ZONE_ROWS[zone] - nd * nh * WIN)), constant_values=-1))
    row = jnp.concatenate(parts, axis=1)
    row = jnp.pad(row, ((0, 0), (0, ROWS - row.shape[1])), constant_values=-1)
    return row.reshape(2, 1, ROWS).astype(F32)


def shards(
    volume,
    patch_mask,
    mask_token,
    labels,
    norm_gain,
    qkv_weight,
    proj_weight,
    merge_gain,
    merge_weight,
    upstream,
):
    sizes = tuple(lax.axis_size(n) for n in ("depth", "height", "batch"))
    pick = slab_to_pieces()
    mask = jnp.pad(patch_mask[0], ((0, 0), (0, 0), (0, PITCH - EDGE))).reshape(EDGE, 1, SLAB).astype(BF16)
    label = jnp.concatenate([group_labels(labels[0], group) for group in GROUP_LIST], 0)
    params = jnp.concatenate((norm_gain, mask_token.astype(F32), merge_gain)).reshape(10, C)
    operands = (
        volume,
        upstream,
        mask,
        label,
        jnp.asarray(pick, BF16),
        jnp.asarray(pick.T, BF16),
        jnp.asarray(slab_to_cells(), BF16),
        params,
        qkv_weight,
        proj_weight,
        jnp.asarray(np.eye(ATTN), BF16),
        merge_weight.reshape(sizes[2], -1, C),
    )
    merged, grad_qkv, grad_proj = run_block(operands, sizes)
    merged = merged.reshape(2, 7, 7, 8, C)[:, :, :, :7].transpose(1, 0, 2, 3, 4).reshape(1, 7, 14, 7, C)
    return (merged, grad_qkv, grad_proj)


def solution(mesh):
    return jax.shard_map(
        shards,
        mesh=mesh,
        in_specs=(
            P("batch", "depth", "height", None, None),
            P("batch", "depth", "height", None),
            P(),
            P("batch", "depth", "height", None),
            P(),
            P(),
            P(),
            P(),
            P(None, "height"),
            P("batch", "depth", "height", None, None),
        ),
        out_specs=(
            P("batch", "depth", None, None, "height"),
            P(("depth", "height"), None),
            P(("depth", "height"), None),
        ),
        check_vma=False,
    )
```

time: 176 us -> 144 us (0.82)
  between operations: 14.4 us -> 0.9 us
  Pallas kernels: 138 us -> 131 us
  local copies, waits for them, and re-layouts: 13.6 us -> 8.3 us
  starting transfers between devices: 4.14 us -> 0 us
    pallas_call x3 -> x1, Pallas kernels: 138 us -> 131 us  [run_block(): pl.pallas_call(functools.partial(block_kernel, sizes), out_shape=[jax.Sha...]
    ppermute x2 -> x0, starting transfers between devices: 4.1 us -> none  [shifted(): return lax.ppermute(array, axes if len(axes) > 1 else axes[0], pairs)]
    reshape x5 -> x1, local copies, waits for them, and re-layouts: 3.59 us -> 0.61 us  [shards(): jnp.concatenate((norm_gain, mask_token.astype(F32), merge_gain))]
    transpose x1 -> x2, local copies, waits for them, and re-layouts: 0.26 us -> 2.03 us  [shards(): merged.reshape(2, 7, 7, 8, C)[:, :, :, :7].transpose(1, 0, 2, 3, 4)]
    unnamed x19 -> x11, local copies, waits for them, and re-layouts: 4.1 us -> 3.14 us
  transfers between devices with their start and end apart: 3 -> 0, of which waited for: 0 -> 0; matrix products, arithmetic and copies ran while one was open for 8% -> 0% of each run, Pallas kernels for 71% -> 0%
where the time goes in v1:
time: 144 us
  Pallas kernels  131 us (91%)
  local copies, waits for them, and re-layouts  8.3 us (6%)
  other arithmetic  3.29 us (2%)
    pallas_call x1, Pallas kernels, run_block(): pl.pallas_call(functools.partial(block_kernel, sizes), out_shape=[jax.Sha...  131 us
    unnamed x11, local copies, waits for them, and re-layouts  3.14 us

profile of v1, /device:TPU:1, one launch (start us, length us, event | category | flops | bytes accessed | tf_op | source)
XLA Modules:
  0.0 143.6 jit_solution(14625805218020493637)
XLA Ops:
  0.6 0.0 copy-start
  0.6 0.7 convert_element_type.39
  1.4 0.7 pad_maximum_fusion
  2.1 0.6 reshape.112.refs_7_
  2.7 1.0 convert.5
  3.7 0.7 convert_element_type.40.refs_2_
  4.4 0.9 copy.52
  5.3 0.1 reshape.110
  5.4 0.1 reshape.111
  5.5 0.1 reshape.108
  5.6 0.1 reshape.109
  5.7 0.1 reshape.106
  5.8 0.1 reshape.107
  5.9 0.1 reshape.104
  6.0 0.1 reshape.105
  6.1 0.1 fusion.2
  6.2 0.1 reshape.102
  6.3 0.1 reshape.103
  6.5 0.1 reshape.98
  6.6 0.1 reshape.99
  6.7 0.1 reshape.96
  6.8 0.1 reshape.97
  6.9 0.1 select_add_fusion.1
  7.0 0.1 reshape.100
  7.1 0.1 reshape.101
  7.2 0.1 select_add_fusion
  7.3 0.1 reshape.94
  7.4 0.1 reshape.95
  7.6 0.6 pad_maximum_fusion.1.refs_3_
  8.2 0.0 copy-done
  8.2 1.0 copy.41.refs_8_
  9.2 131.1 %block.1 = (bf16[2,392,384]{2,1,0:T(8,128)(2,1)}, f32[12,576]{1,0:T(8,128)}, f32[6,384]{1,0:T(8,128)}) custom-call(bf16[1,14,14,14,384]{4,3,2,1,0:T(8,128)(2,1)} %refs_0_.1, bf16[1,14,14,14,384]{4,3,2,1,0:T(8,128)(2,1)} %refs_1_.1, bf16[14,1,224]{2,1,0:T(2,128)(2,1)} %convert_element_type.40.refs_2_, f32[8,1,384]{2,1,0:T(1,128)} %pad_maximum_fusion.1.refs_3_, ...), custom_call_target="tpu_custom_call" | custom-call | flops 80000000000 | bytes 12000000 | tf_op jit(solution)/shard_map/block/pallas_call | solution.py:433
  140.3 0.0 copy-start.1
  140.3 0.0 copy-start.2
  140.3 1.1 slice_bitcast_fusion
  141.5 0.9 copy.42
  142.3 0.0 copy-done.1
  142.3 0.6 copy.61
  143.0 0.0 copy-done.2
  143.0 0.6 copy.62
  (31 shorter events, 0.2 us)
Async XLA Ops:
  0.6 7.6 %copy-start = (bf16[384,576]{0,1:T(8,128)(2,1)S(1)}, bf16[384,576]{0,1:T(8,128)(2,1)}, u32[]{:S(2)}) copy-start(bf16[384,576]{0,1:T(8,128)(2,1)} %param.19) | copy-start | bytes 1327108
  140.3 2.1 %copy-start.1 = (f32[12,576]{1,0:T(8,128)S(1)}, f32[12,576]{1,0:T(8,128)}, u32[]{:S(2)}) copy-start(f32[12,576]{1,0:T(8,128)} %get-tuple-element.13) | copy-start | bytes 82948
  140.3 2.7 %copy-start.2 = (f32[6,384]{1,0:T(8,128)S(1)}, f32[6,384]{1,0:T(8,128)}, u32[]{:S(2)}) copy-start(f32[6,384]{1,0:T(8,128)} %get-tuple-element.14) | copy-start | bytes 27652

commit v2 on v1

--- a/solution.py
+++ b/solution.py
@@ -126,18 +126,29 @@
     merged_out, grad_qkv_out, grad_proj_out = refs[12:15]
     x, space, pad_v, pad_u, context_w, context_z, bias, proj, proj_t, dcon_t, con_t, dproj_t = refs[15:27]
     weight_t, grad, context_space, context_all, features, other, sent, fetched = refs[27:35]
-    terms, arrived, total, gathered, ahead_send, ahead_recv, back_send, back_recv = refs[35:43]
-    share_send, share_recv, merged_send, merged_recv = refs[43:47]
-    term_send, term_recv, sum_send, sum_recv = refs[47:51]
-    send_buffers = dict(zip(HALO, refs[51:56]))
+    terms, landed, partial, ahead_send, ahead_recv, back_send, back_recv = refs[35:42]
+    share_send, share_recv, merged_send, merged_recv, term_send, term_recv = refs[42:48]
+    send_buffers = dict(zip(HALO, refs[48:53]))
 
     depth, height, batch = (lax.axis_index(n) for n in ("depth", "height", "batch"))
     me = depth * heights + height
     peer = {"height": heights - 1 - height}
 
+    across = min(depths, 4)
+    planes = owners // across
+    across_at = lax.rem(depth, across)
+    plane_at = depth // across * heights + height
+
     def owner_at(step):
         to = lax.rem(me + step, owners)
         return {"depth": to // heights, "height": lax.rem(to, heights)}
+
+    def member(stage, place):
+        if stage == 0:
+            return {"depth": depth // across * across + place}
+        if stage == 1:
+            return {"depth": place // heights * across + across_at, "height": lax.rem(place, heights)}
+        return {"batch": place}
 
     def batch_at(step):
         return {"batch": lax.rem(batch + step, batches)}
@@ -169,23 +180,49 @@
     def first_share():
         return remote(own.at[batch], other.at[0], share_send.at[0], share_recv.at[0], peer)
 
+    def pass_share():
+        before = {"depth": lax.rem(depth + depths - 1, depths)}
+        return remote(other.at[0], other.at[0], share_send.at[batches], share_recv.at[0], before)
+
     def next_share(step):
         return remote(other.at[0], other.at[step], share_send.at[step], share_recv.at[step], batch_at(step))
 
     def swap_merged():
         return remote(sent, fetched, merged_send.at[0], merged_recv.at[0], peer)
 
-    def term(kind, step):
+    places = (across_at, plane_at, batch)
+    counts = (across, planes, batches)
+
+    def exchange(stage, kind, step):
+        place = lax.rem(places[stage] + step, counts[stage])
+        source = (terms[kind].at[place], partial[0][kind].at[place], partial[1][kind])[stage]
+        slot = sum(counts[:stage]) + step
         return remote(
-            terms[kind].at[lax.rem(me + step, owners)],
-            arrived[kind].at[step],
-            term_send.at[kind, step],
-            term_recv.at[kind, step],
-            owner_at(step),
+            source,
+            landed[stage][kind].at[step],
+            term_send.at[kind, slot],
+            term_recv.at[kind, slot],
+            member(stage, place),
         )
 
-    def to_batch(step):
-        return remote(total, gathered.at[step], sum_send.at[step], sum_recv.at[step], batch_at(step))
+    def begin(stage, kind):
+        @pl.loop(1, counts[stage])
+        def _(step):
+            exchange(stage, kind, step).start()
+
+    def finish(stage, kind):
+        out = partial[stage][kind]
+        if stage == 0:
+            out[...] = terms[kind][across_at].astype(F32)
+        elif stage == 1:
+            out[...] = partial[0][kind][plane_at]
+        else:
+            out[...] = partial[1][kind][...]
+
+        @pl.loop(1, counts[stage])
+        def _(step):
+            exchange(stage, kind, step).wait_recv()
+            out[...] += landed[stage][kind][step].astype(F32)
 
     barrier = pltpu.get_barrier_semaphore()
 
@@ -234,12 +271,15 @@
                 else:
                     group = GROUP_LIST.index(((dz - 1), (hz - 1)))
                     x[2 * group : 2 * group + 2, 0:rows, :] = filled
-    first_share().start()
+    late = 1 - (lax.rem(depth, 4) + 3) // 4
+
+    @pl.when(late == 0)
+    def _():
+        first_share().start()
 
     weight_t[...] = jnp.transpose(weight[...].astype(F32)).astype(BF16)
     grad[...] = jnp.zeros_like(grad)
     scale = HEAD**-0.5
-    late = 1 - (lax.rem(depth, 4) + 3) // 4
 
     @pl.loop(0, 8)
     def _(turn):
@@ -254,9 +294,13 @@
                         if zone in AHEAD:
                             ahead(zone).wait_recv()
 
-        @pl.when(turn == 3)
+        @pl.when(turn == 3 + 2 * late)
         def _():
             first_share().wait_recv()
+
+            @pl.when(lax.rem(depth, 4) == 1)
+            def _():
+                pass_share().start()
 
             @pl.loop(1, batches)
             def _(step):
@@ -295,38 +339,56 @@
                             if zone in AHEAD:
                                 back(zone, half).start()
 
+    def place_of(owner):
+        return owner // heights % across, owner // heights // across * heights + owner % heights
+
     spread = jnp.transpose(grad[...])
     terms[0][...] = jnp.zeros_like(terms[0])
     for o in range(owners):
-        terms[0][o, 0:lines, 0 : 3 * ATTN] = spread[o * lines : (o + 1) * lines].astype(BF16)
-
-    @pl.loop(1, owners)
-    def _(step):
-        term(0, step).start()
+        terms[0][*place_of(o), 0:lines, 0 : 3 * ATTN] = spread[o * lines : (o + 1) * lines].astype(BF16)
+    begin(0, 0)
 
     for zone in ZONES:
         if zone not in AHEAD:
             group = GROUP_LIST.index((zone[0] - 1, zone[1] - 1))
             base, rows = ZONE_BASE[zone], ZONE_ROWS[zone]
             context_z[:, base : base + rows, :] = context_w[2 * group : 2 * group + 2, 0:rows, :]
-    for zone in HALO:
-        for half in range(2):
-            back(zone, half).wait_recv()
     context_space[:, TOTAL:, :] = jnp.zeros((2, context_space.shape[1] - TOTAL, ATTN), F32)
-    context_space[:, 0:TOTAL, :] = context_z[...].astype(F32)
-    for pair in range(EDGE // 2):
-        blocks = []
-        for d in (2 * pair, 2 * pair + 1):
-            dz, at = zone_of(d)
-            for h in range(EDGE):
-                pad_v[d % 2, h, 0:EDGE, :] = vol[0, d, h]
+
+    def restore(dz):
+        start, stop = ZONE_BASE[(dz, 0)], ZONE_BASE[(dz, 2)] + ZONE_ROWS[(dz, 2)]
+        context_space[:, start:stop, :] = context_z[:, start:stop, :].astype(F32)
+        for at in range(SIZES[dz]):
+            d = FIRST[dz] + at
             pieces = []
             for half, hz, _ in PIECES:
                 row = ZONE_BASE[(dz, hz)] + at * WIN * SIZES[hz]
                 pieces.append(context_space[half, row : row + PIECE_ROWS[hz], :])
-            context = nn(back_pick[...], jnp.concatenate(pieces, axis=0).astype(BF16)).astype(BF16)
-            context_all[d * SLAB : (d + 1) * SLAB, :] = context
-            attended = nn(context, weight_p[...]).astype(BF16)
+            context = nn(back_pick[...], jnp.concatenate(pieces, axis=0).astype(BF16))
+            context_all[d * SLAB : (d + 1) * SLAB, :] = context.astype(BF16)
+
+    for dz in (1, 2, 0):
+        for zone in HALO:
+            if zone[0] == dz:
+                for half in range(2):
+                    back(zone, half).wait_recv()
+        restore(dz)
+
+    grad_proj = tn(context_all[...], pad_u[...].reshape(EDGE * SLAB, C))
+    terms[1][...] = jnp.zeros_like(terms[1])
+    per = ATTN // owners
+    for o in range(owners):
+        rows = grad_proj[o * per : (o + 1) * per].astype(BF16)
+        terms[1][*place_of(o), 0:per, 0:ATTN] = rows[:, 0:ATTN]
+        terms[1][*place_of(o), per : 2 * per, 0:ATTN] = rows[:, ATTN:]
+    begin(0, 1)
+
+    def merge_pair(pair):
+        blocks = []
+        for d in (2 * pair, 2 * pair + 1):
+            for h in range(EDGE):
+                pad_v[d % 2, h, 0:EDGE, :] = vol[0, d, h]
+            attended = nn(context_all[d * SLAB : (d + 1) * SLAB, :], weight_p[...]).astype(BF16)
             shown, hidden = masked_pick(cells[...], mask[d])
             tokens = nn(shown, pad_v[d % 2].reshape(SLAB, C)) + hidden * token
             block = (tokens + nn(cells[...], attended)).astype(BF16).astype(F32)
@@ -340,17 +402,14 @@
         for o in range(8):
             features[o, pair * 56 : pair * 56 + 56, :] = centered[o] * factor * params[2 + o : 3 + o, :]
 
-    grad_proj = tn(context_all[...], pad_u[...].reshape(EDGE * SLAB, C))
-    terms[1][...] = jnp.zeros_like(terms[1])
-    per = ATTN // owners
-    for o in range(owners):
-        rows = grad_proj[o * per : (o + 1) * per].astype(BF16)
-        terms[1][o, 0:per, 0:ATTN] = rows[:, 0:ATTN]
-        terms[1][o, per : 2 * per, 0:ATTN] = rows[:, ATTN:]
-
-    @pl.loop(1, owners)
-    def _(step):
-        term(1, step).start()
+    for pair in range(4):
+        merge_pair(pair)
+    finish(0, 0)
+    begin(1, 0)
+    for pair in range(4, EDGE // 2):
+        merge_pair(pair)
+    finish(0, 1)
+    begin(1, 1)
 
     @pl.loop(1, batches)
     def _(step):
@@ -365,59 +424,48 @@
     sent[0 : result.shape[0], :] = result.astype(BF16)
     sent[result.shape[0] :, :] = jnp.zeros((sent.shape[0] - result.shape[0], C), BF16)
     swap_merged().start()
+    for kind in range(2):
+        finish(1, kind)
+        begin(2, kind)
     result = jnp.zeros(features.shape[1:], F32)
     for step in range(batches):
         for k in range(each):
             result += nn(features[step * each + k].astype(BF16), own[step, k * C : (k + 1) * C, :])
     merged_out[height] = result.astype(BF16)
-
-    wide = terms[0].shape[2]
-    total[:, 0:wide] = terms[0][me].astype(F32)
-    total[:, wide:] = terms[1][me].astype(F32)
-
-    @pl.loop(1, owners)
-    def _(step):
-        term(0, step).wait_recv()
-        total[:, 0:wide] += arrived[0][step].astype(F32)
-
-    @pl.loop(1, owners)
-    def _(step):
-        term(1, step).wait_recv()
-        total[:, wide:] += arrived[1][step].astype(F32)
-
-    @pl.loop(1, batches)
-    def _(step):
-        to_batch(step).start()
-
+    for kind in range(2):
+        finish(2, kind)
+    sums = partial[2]
+    grad_qkv_out[...] = sums[0][0:lines, 0 : 3 * ATTN]
+    grad_proj_out[:, 0:ATTN] = sums[1][0:per, 0:ATTN]
+    grad_proj_out[:, ATTN:] = sums[1][per : 2 * per, 0:ATTN]
     swap_merged().wait_recv()
     merged_out[heights - 1 - height] = fetched[0 : result.shape[0], :]
-    gathered[0] = total[...]
-
-    @pl.loop(1, batches)
-    def _(step):
-        to_batch(step).wait_recv()
-        gathered[0] += gathered[step]
-
-    grad_qkv_out[...] = gathered[0, 0:lines, 0 : 3 * ATTN]
-    grad_proj_out[:, 0:ATTN] = gathered[0, 0:per, wide : wide + ATTN]
-    grad_proj_out[:, ATTN:] = gathered[0, per : 2 * per, wide : wide + ATTN]
 
     for zone in HALO:
         ahead(zone).wait_send()
         for half in range(2):
             back(zone, half).wait_send()
-    first_share().wait_send()
+
+    @pl.when(late == 0)
+    def _():
+        first_share().wait_send()
+
+    @pl.when(lax.rem(depth, 4) == 1)
+    def _():
+        pass_share().wait_send()
+
     swap_merged().wait_send()
-
-    @pl.loop(1, owners)
-    def _(step):
-        term(0, step).wait_send()
-        term(1, step).wait_send()
 
     @pl.loop(1, batches)
     def _(step):
         next_share(step).wait_send()
-        to_batch(step).wait_send()
+
+    for stage in range(3):
+        for kind in range(2):
+
+            @pl.loop(1, counts[stage])
+            def _(step):
+                exchange(stage, kind, step).wait_send()
 
 
 def run_block(operands, sizes):
@@ -427,8 +475,13 @@
     wide, narrow = up(3 * ATTN, 128), up(ATTN, 128)
     cell_rows = 7 * 56
 
-    def pair_of(rows):
-        return [pltpu.VMEM((rows, lines, wide), BF16), pltpu.VMEM((rows, lines, narrow), BF16)]
+    across = min(sizes[0], 4)
+    planes = owners // across
+
+    def pair_of(kind, *shape):
+        return [pltpu.VMEM(shape + (lines, wide), kind), pltpu.VMEM(shape + (lines, narrow), kind)]
+
+    exchanges = across + planes + batches
 
     return pl.pallas_call(
         functools.partial(block_kernel, sizes),
@@ -460,22 +513,19 @@
             pltpu.VMEM((batches, 8 * C // batches, C), BF16),
             pltpu.VMEM((up(cell_rows, 16), C), BF16),
             pltpu.VMEM((up(cell_rows, 16), C), BF16),
-            pair_of(owners),
-            pair_of(owners),
-            pltpu.VMEM((lines, wide + narrow), F32),
-            pltpu.VMEM((batches, lines, wide + narrow), F32),
+            pair_of(BF16, across, planes),
+            [pair_of(BF16, across, planes), pair_of(F32, planes), pair_of(F32, batches)],
+            [pair_of(F32, planes), pair_of(F32), pair_of(F32)],
             pltpu.SemaphoreType.DMA((5,)),
             pltpu.SemaphoreType.DMA((5,)),
             pltpu.SemaphoreType.DMA((10,)),
             pltpu.SemaphoreType.DMA((10,)),
-            pltpu.SemaphoreType.DMA((batches,)),
+            pltpu.SemaphoreType.DMA((batches + 1,)),
             pltpu.SemaphoreType.DMA((batches,)),
             pltpu.SemaphoreType.DMA((1,)),
             pltpu.SemaphoreType.DMA((1,)),
-            pltpu.SemaphoreType.DMA((2, owners)),
-            pltpu.SemaphoreType.DMA((2, owners)),
-            pltpu.SemaphoreType.DMA((batches,)),
-            pltpu.SemaphoreType.DMA((batches,)),
+            pltpu.SemaphoreType.DMA((2, exchanges)),
+            pltpu.SemaphoreType.DMA((2, exchanges)),
         ]
         + [pltpu.VMEM((2, ZONE_ROWS[zone], FEED), BF16) for zone in HALO],
         cost_estimate=pl.CostEstimate(flops=80_000_000_000, bytes_accessed=12_000_000, transcendentals=8_000_000),

time: 144 us -> 124 us (0.86)
  Pallas kernels: 131 us -> 110 us
    pallas_call x1, Pallas kernels: 131 us -> 110 us  [run_block(): pl.pallas_call(functools.partial(block_kernel, sizes), out_shape=[jax.Sha...]
where the time goes in v2:
time: 124 us; the launch traced here: 123 us
  Pallas kernels  110 us (89%)
  local copies, waits for them, and re-layouts  8.3 us (7%)
  other arithmetic  3.29 us (3%)
    pallas_call x1, Pallas kernels, run_block(): pl.pallas_call(functools.partial(block_kernel, sizes), out_shape=[jax.Sha...  110 us
    unnamed x11, local copies, waits for them, and re-layouts  3.14 us

profile of v2, /device:TPU:1, one launch (start us, length us, event | category | flops | bytes accessed | tf_op | source)
XLA Modules:
  0.0 122.7 jit_solution(10479354176540339129)
XLA Ops:
  0.6 0.0 copy-start
  0.6 0.7 convert_element_type.39
  1.4 0.7 pad_maximum_fusion
  2.1 0.6 reshape.112.refs_7_
  2.7 1.0 convert.5
  3.7 0.7 convert_element_type.40.refs_2_
  4.4 0.9 copy.52
  5.3 0.1 reshape.110
  5.4 0.1 reshape.111
  5.5 0.1 reshape.108
  5.6 0.1 reshape.109
  5.7 0.1 reshape.106
  5.8 0.1 reshape.107
  5.9 0.1 reshape.104
  6.0 0.1 reshape.105
  6.1 0.1 fusion.2
  6.2 0.1 reshape.102
  6.3 0.1 reshape.103
  6.5 0.1 reshape.98
  6.6 0.1 reshape.99
  6.7 0.1 reshape.96
  6.8 0.1 reshape.97
  6.9 0.1 select_add_fusion.1
  7.0 0.1 reshape.100
  7.1 0.1 reshape.101
  7.2 0.1 select_add_fusion
  7.3 0.1 reshape.94
  7.4 0.1 reshape.95
  7.6 0.6 pad_maximum_fusion.1.refs_3_
  8.2 0.0 copy-done
  8.2 1.0 copy.41.refs_8_
  9.2 110.2 %block.1 = (bf16[2,392,384]{2,1,0:T(8,128)(2,1)}, f32[12,576]{1,0:T(8,128)}, f32[6,384]{1,0:T(8,128)}) custom-call(bf16[1,14,14,14,384]{4,3,2,1,0:T(8,128)(2,1)} %refs_0_.1, bf16[1,14,14,14,384]{4,3,2,1,0:T(8,128)(2,1)} %refs_1_.1, bf16[14,1,224]{2,1,0:T(2,128)(2,1)} %convert_element_type.40.refs_2_, f32[8,1,384]{2,1,0:T(1,128)} %pad_maximum_fusion.1.refs_3_, ...), custom_call_target="tpu_custom_call" | custom-call | flops 80000000000 | bytes 12000000 | tf_op jit(solution)/shard_map/block/pallas_call | solution.py:486
  119.4 0.0 copy-start.1
  119.4 0.0 copy-start.2
  119.4 1.1 slice_bitcast_fusion
  120.6 0.9 copy.42
  121.5 0.0 copy-done.1
  121.5 0.6 copy.61
  122.1 0.0 copy-done.2
  122.1 0.6 copy.62
  (31 shorter events, 0.2 us)
Async XLA Ops:
  0.6 7.6 %copy-start = (bf16[384,576]{0,1:T(8,128)(2,1)S(1)}, bf16[384,576]{0,1:T(8,128)(2,1)}, u32[]{:S(2)}) copy-start(bf16[384,576]{0,1:T(8,128)(2,1)} %param.19) | copy-start | bytes 1327108
  119.4 2.1 %copy-start.1 = (f32[12,576]{1,0:T(8,128)S(1)}, f32[12,576]{1,0:T(8,128)}, u32[]{:S(2)}) copy-start(f32[12,576]{1,0:T(8,128)} %get-tuple-element.13) | copy-start | bytes 82948
  119.4 2.7 %copy-start.2 = (f32[6,384]{1,0:T(8,128)S(1)}, f32[6,384]{1,0:T(8,128)}, u32[]{:S(2)}) copy-start(f32[6,384]{1,0:T(8,128)} %get-tuple-element.14) | copy-start | bytes 27652

commit v3 on v2

--- a/solution.py
+++ b/solution.py
@@ -102,6 +102,8 @@
             AHEAD[zone] = (_group, _row)
         _row += ZONE_ROWS[zone]
 HALO = list(AHEAD)
+DEEP = [(0, 1), (0, 2)]
+LATER = [(2, 0), (0, 2), (0, 0)]
 GROUP_LIST = list(GROUPS)
 
 
@@ -122,13 +124,15 @@
     depths, heights, batches = sizes
     owners = depths * heights
     lines = C // owners
-    vol, ups, mask, label, pick, back_pick, cells, params, weight, weight_p, eye, own = refs[:12]
+    vol, ups, mask, label, pick, back_pick, cells, params, weight_t, weight_p, eye, own = refs[:12]
     merged_out, grad_qkv_out, grad_proj_out = refs[12:15]
     x, space, pad_v, pad_u, context_w, context_z, bias, proj, proj_t, dcon_t, con_t, dproj_t = refs[15:27]
-    weight_t, grad, context_space, context_all, features, other, sent, fetched = refs[27:35]
-    terms, landed, partial, ahead_send, ahead_recv, back_send, back_recv = refs[35:42]
-    share_send, share_recv, merged_send, merged_recv, term_send, term_recv = refs[42:48]
-    send_buffers = dict(zip(HALO, refs[48:53]))
+    grad, context_space, context_all, features, other, sent, fetched = refs[27:34]
+    terms, landed, partial, ahead_send, ahead_recv, back_send, back_recv = refs[34:41]
+    share_send, share_recv, merged_send, merged_recv, term_send, term_recv = refs[41:47]
+    send_buffers = dict(zip(HALO, refs[47:52]))
+    score_all, weight_all, dscore_all, weight, relay_send, relay_recv = refs[52:58]
+    relay_buffers = dict(zip(DEEP, refs[58:60]))
 
     depth, height, batch = (lax.axis_index(n) for n in ("depth", "height", "batch"))
     me = depth * heights + height
@@ -158,13 +162,64 @@
             src_ref=src, dst_ref=dst, send_sem=send, recv_sem=recv, device_id=device, device_id_type=MESH
         )
 
-    def ahead(zone):
+    relayed = depths % 4 == 0 and depths > 4
+    along = lax.rem(depth, 4)
+    late = 1 - (along + 3) // 4
+
+    def landing(zone, half):
         group, row = AHEAD[zone]
-        slot = HALO.index(zone)
-        landing = x.at[pl.ds(2 * GROUP_LIST.index(group), 2), pl.ds(row, ZONE_ROWS[zone]), :]
+        return x.at[2 * GROUP_LIST.index(group) + half, pl.ds(row, ZONE_ROWS[zone]), :]
+
+    def ahead(zone, half):
+        slot = 2 * HALO.index(zone) + half
         return remote(
-            send_buffers[zone], landing, ahead_send.at[slot], ahead_recv.at[slot], neighbour(zone, -1, sizes)
+            send_buffers[zone].at[half],
+            landing(zone, half),
+            ahead_send.at[slot],
+            ahead_recv.at[slot],
+            neighbour(zone, -1, sizes),
         )
+
+    def to_relay(zone):
+        slot = DEEP.index(zone)
+        return remote(
+            send_buffers[zone].at[1],
+            relay_buffers[zone],
+            ahead_send.at[2 * HALO.index(zone) + 1],
+            relay_recv.at[slot],
+            {"depth": lax.rem(depth + 3, depths)},
+        )
+
+    def from_relay(zone):
+        return remote(
+            relay_buffers[zone],
+            landing(zone, 1),
+            relay_send.at[DEEP.index(zone)],
+            ahead_recv.at[2 * HALO.index(zone) + 1],
+            {"depth": lax.rem(depth + depths - 4, depths)},
+        )
+
+    def send_ahead(zone):
+        ahead(zone, 0).start()
+        if relayed and zone in DEEP:
+
+            @pl.when(late == 1)
+            def _():
+                to_relay(zone).start()
+
+            @pl.when(late == 0)
+            def _():
+                ahead(zone, 1).start()
+        else:
+            ahead(zone, 1).start()
+
+    def pass_on(zone):
+        if relayed:
+
+            @pl.when(along == 3)
+            def _():
+                to_relay(zone).wait_recv()
+                from_relay(zone).start()
 
     def back(zone, half):
         group, row = AHEAD[zone]
@@ -244,10 +299,10 @@
     for d in range(EDGE):
         dz, at = zone_of(d)
         for h in range(EDGE):
-            pad_v[d % 2, h, 0:EDGE, :] = vol[0, d, h]
+            pad_v[d, h, 0:EDGE, :] = vol[0, d, h]
             pad_u[d, h, 0:EDGE, :] = ups[0, d, h]
         shown, hidden = masked_pick(pick[...], mask[d])
-        tokens = nn(shown, pad_v[d % 2].reshape(SLAB, C)) + hidden * token
+        tokens = nn(shown, pad_v[d].reshape(SLAB, C)) + hidden * token
         mean = jnp.mean(tokens, axis=1, keepdims=True)
         centered = tokens - mean
         variance = jnp.mean(centered * centered, axis=1, keepdims=True)
@@ -267,17 +322,16 @@
                 filled = space[:, base : base + rows, :].astype(BF16)
                 if zone in AHEAD:
                     send_buffers[zone][...] = filled
-                    ahead(zone).start()
+                    if zone not in LATER:
+                        send_ahead(zone)
                 else:
                     group = GROUP_LIST.index(((dz - 1), (hz - 1)))
                     x[2 * group : 2 * group + 2, 0:rows, :] = filled
-    late = 1 - (lax.rem(depth, 4) + 3) // 4
-
     @pl.when(late == 0)
     def _():
         first_share().start()
 
-    weight_t[...] = jnp.transpose(weight[...].astype(F32)).astype(BF16)
+    weight[...] = jnp.transpose(weight_t[...].astype(F32)).astype(BF16)
     grad[...] = jnp.zeros_like(grad)
     scale = HEAD**-0.5
 
@@ -292,7 +346,21 @@
                 def _():
                     for zone in GROUPS[group]:
                         if zone in AHEAD:
-                            ahead(zone).wait_recv()
+                            ahead(zone, 0).wait_recv()
+                            ahead(zone, 1).wait_recv()
+
+        @pl.when(turn == 0)
+        def _():
+            pass_on(DEEP[0])
+
+        @pl.when(turn == 1)
+        def _():
+            for zone in LATER:
+                send_ahead(zone)
+
+        @pl.when(turn == 3)
+        def _():
+            pass_on(DEEP[1])
 
         @pl.when(turn == 3 + 2 * late)
         def _():
@@ -313,20 +381,23 @@
         proj[...] = nn(normed, weight[...]).astype(BF16)
         proj_t[...] = nt(weight_t[...], normed).astype(BF16)
         dcon_t[...] = nt(eye[...], x[i, :, C:FEED]).astype(BF16)
-        for head in range(HEADS):
-            a, b, c = (slice(k * ATTN + head * HEAD, k * ATTN + head * HEAD + HEAD) for k in range(3))
-            scores = nn(proj[:, b], proj_t[a, :]) * (scale * math.log2(math.e)) + bias[...]
+        parts = [[slice(k * ATTN + h * HEAD, k * ATTN + h * HEAD + HEAD) for k in range(3)] for h in range(HEADS)]
+        for head, (a, b, c) in enumerate(parts):
+            score_all[head] = nn(proj[:, b], proj_t[a, :]) * (scale * math.log2(math.e)) + bias[...]
+        for head, (a, b, c) in enumerate(parts):
+            scores = score_all[head]
             exponent = jnp.exp2(scores - jnp.max(scores, axis=0, keepdims=True))
-            weights = (exponent * (1.0 / jnp.sum(exponent, axis=0, keepdims=True))).astype(BF16)
-            context_t = nn(proj_t[c, :], weights)
-            con_t[a, :] = context_t
-            inner = jnp.sum(dcon_t[a, :].astype(F32) * context_t, axis=0, keepdims=True)
+            weight_all[head] = (exponent * (1.0 / jnp.sum(exponent, axis=0, keepdims=True))).astype(BF16)
+            con_t[a, :] = nn(proj_t[c, :], weight_all[head])
+            cot = x[i, :, C + head * HEAD : C + head * HEAD + HEAD]
+            dproj_t[c, :] = jnp.transpose(nn(weight_all[head], cot)).astype(BF16)
+        for head, (a, b, c) in enumerate(parts):
+            inner = jnp.sum(dcon_t[a, :].astype(F32) * con_t[a, :], axis=0, keepdims=True)
             dweights = nn(proj[:, c], dcon_t[a, :])
-            dscores = (weights.astype(F32) * (dweights - inner) * scale).astype(BF16)
-            dproj_t[a, :] = nn(proj_t[b, :], dscores).astype(BF16)
-            dproj_t[b, :] = jnp.transpose(nn(dscores, proj[:, a])).astype(BF16)
-            cot = x[i, :, C + head * HEAD : C + head * HEAD + HEAD]
-            dproj_t[c, :] = jnp.transpose(nn(weights, cot)).astype(BF16)
+            dscore_all[head] = (weight_all[head].astype(F32) * (dweights - inner) * scale).astype(BF16)
+        for head, (a, b, c) in enumerate(parts):
+            dproj_t[a, :] = nn(proj_t[b, :], dscore_all[head]).astype(BF16)
+            dproj_t[b, :] = jnp.transpose(nn(dscore_all[head], proj[:, a])).astype(BF16)
         context_w[i] = jnp.transpose(con_t[...]).astype(BF16)
         grad[...] += nn(dproj_t[...], normed)
         for number, group in enumerate(GROUP_LIST):
@@ -386,11 +457,9 @@
     def merge_pair(pair):
         blocks = []
         for d in (2 * pair, 2 * pair + 1):
-            for h in range(EDGE):
-                pad_v[d % 2, h, 0:EDGE, :] = vol[0, d, h]
             attended = nn(context_all[d * SLAB : (d + 1) * SLAB, :], weight_p[...]).astype(BF16)
             shown, hidden = masked_pick(cells[...], mask[d])
-            tokens = nn(shown, pad_v[d % 2].reshape(SLAB, C)) + hidden * token
+            tokens = nn(shown, pad_v[d].reshape(SLAB, C)) + hidden * token
             block = (tokens + nn(cells[...], attended)).astype(BF16).astype(F32)
             blocks += [block[o * 56 : o * 56 + 56] for o in range(4)]
         summed = sum(blocks[1:], blocks[0])
@@ -442,9 +511,15 @@
     merged_out[heights - 1 - height] = fetched[0 : result.shape[0], :]
 
     for zone in HALO:
-        ahead(zone).wait_send()
         for half in range(2):
+            ahead(zone, half).wait_send()
             back(zone, half).wait_send()
+    if relayed:
+
+        @pl.when(along == 3)
+        def _():
+            for zone in DEEP:
+                from_relay(zone).wait_send()
 
     @pl.when(late == 0)
     def _():
@@ -495,7 +570,7 @@
         scratch_shapes=[
             pltpu.VMEM((8, ROWS, FEED), BF16),
             pltpu.VMEM((2, TOTAL, FEED), F32),
-            pltpu.VMEM((2, EDGE, PITCH, C), BF16),
+            pltpu.VMEM((EDGE, EDGE, PITCH, C), BF16),
             pltpu.VMEM((EDGE, EDGE, PITCH, C), BF16),
             pltpu.VMEM((8, ROWS, ATTN), BF16),
             pltpu.VMEM((2, TOTAL, ATTN), BF16),
@@ -505,7 +580,6 @@
             pltpu.VMEM((ATTN, ROWS), BF16),
             pltpu.VMEM((ATTN, ROWS), F32),
             pltpu.VMEM((3 * ATTN, ROWS), BF16),
-            pltpu.VMEM((3 * ATTN, C), BF16),
             pltpu.VMEM((3 * ATTN, C), F32),
             pltpu.VMEM((2, TOTAL + 32, ATTN), F32),
             pltpu.VMEM((EDGE * SLAB, ATTN), BF16),
@@ -516,8 +590,8 @@
             pair_of(BF16, across, planes),
             [pair_of(BF16, across, planes), pair_of(F32, planes), pair_of(F32, batches)],
             [pair_of(F32, planes), pair_of(F32), pair_of(F32)],
-            pltpu.SemaphoreType.DMA((5,)),
-            pltpu.SemaphoreType.DMA((5,)),
+            pltpu.SemaphoreType.DMA((10,)),
+            pltpu.SemaphoreType.DMA((10,)),
             pltpu.SemaphoreType.DMA((10,)),
             pltpu.SemaphoreType.DMA((10,)),
             pltpu.SemaphoreType.DMA((batches + 1,)),
@@ -527,7 +601,16 @@
             pltpu.SemaphoreType.DMA((2, exchanges)),
             pltpu.SemaphoreType.DMA((2, exchanges)),
         ]
-        + [pltpu.VMEM((2, ZONE_ROWS[zone], FEED), BF16) for zone in HALO],
+        + [pltpu.VMEM((2, ZONE_ROWS[zone], FEED), BF16) for zone in HALO]
+        + [
+            pltpu.VMEM((HEADS, ROWS, ROWS), F32),
+            pltpu.VMEM((HEADS, ROWS, ROWS), BF16),
+            pltpu.VMEM((HEADS, ROWS, ROWS), BF16),
+            pltpu.VMEM((C, 3 * ATTN), BF16),
+            pltpu.SemaphoreType.DMA((2,)),
+            pltpu.SemaphoreType.DMA((2,)),
+        ]
+        + [pltpu.VMEM((ZONE_ROWS[zone], FEED), BF16) for zone in DEEP],
         cost_estimate=pl.CostEstimate(flops=80_000_000_000, bytes_accessed=12_000_000, transcendentals=8_000_000),
         compiler_params=pltpu.CompilerParams(
             collective_id=1, has_side_effects=True, vmem_limit_bytes=VMEM_LIMIT
@@ -578,7 +661,7 @@
         jnp.asarray(pick.T, BF16),
         jnp.asarray(slab_to_cells(), BF16),
         params,
-        qkv_weight,
+        qkv_weight.T,
         proj_weight,
         jnp.asarray(np.eye(ATTN), BF16),
         merge_weight.reshape(sizes[2], -1, C),

time: 124 us -> 109 us (0.88); the launches traced: 123 us -> 109 us
  Pallas kernels: 110 us -> 97.7 us
    pallas_call x1, Pallas kernels: 110 us -> 97.7 us  [run_block(): pl.pallas_call(functools.partial(block_kernel, sizes), out_shape=[jax.Sha...]
    unnamed x11 -> x8, local copies, waits for them, and re-layouts: 3.14 us -> 2.14 us
where the time goes in v3:
time: 109 us
  Pallas kernels  97.7 us (90%)
  local copies, waits for them, and re-layouts  7.3 us (7%)
  other arithmetic  3.24 us (3%)
    pallas_call x1, Pallas kernels, run_block(): pl.pallas_call(functools.partial(block_kernel, sizes), out_shape=[jax.Sha...  97.7 us

profile of v3, /device:TPU:1, one launch (start us, length us, event | category | flops | bytes accessed | tf_op | source)
XLA Modules:
  0.0 109.1 jit_solution(17867887476449468578)
XLA Ops:
  0.6 0.7 convert_element_type.39
  1.3 0.7 pad_maximum_fusion
  2.0 0.6 reshape.112.refs_7_
  2.6 1.0 convert.5
  3.7 0.7 convert_element_type.40.refs_2_
  4.4 0.9 copy.50
  5.3 0.1 reshape.110
  5.4 0.1 reshape.111
  5.5 0.1 reshape.108
  5.6 0.1 reshape.109
  5.7 0.1 reshape.106
  5.8 0.1 reshape.107
  5.9 0.1 reshape.104
  6.0 0.1 reshape.105
  6.1 0.1 fusion.2
  6.2 0.1 reshape.102
  6.3 0.1 reshape.103
  6.4 0.1 reshape.98
  6.5 0.1 reshape.99
  6.6 0.1 reshape.96
  6.7 0.1 reshape.97
  6.8 0.1 select_add_fusion.1
  7.0 0.1 reshape.100
  7.1 0.1 reshape.101
  7.2 0.1 select_add_fusion
  7.3 0.1 reshape.94
  7.4 0.1 reshape.95
  7.5 0.6 pad_maximum_fusion.1.refs_3_
  8.1 97.7 %block.1 = (bf16[2,392,384]{2,1,0:T(8,128)(2,1)}, f32[12,576]{1,0:T(8,128)}, f32[6,384]{1,0:T(8,128)}) custom-call(bf16[1,14,14,14,384]{4,3,2,1,0:T(8,128)(2,1)} %refs_0_.1, bf16[1,14,14,14,384]{4,3,2,1,0:T(8,128)(2,1)} %refs_1_.1, bf16[14,1,224]{2,1,0:T(2,128)(2,1)} %convert_element_type.40.refs_2_, f32[8,1,384]{2,1,0:T(1,128)} %pad_maximum_fusion.1.refs_3_, ...), custom_call_target="tpu_custom_call" | custom-call | flops 80000000000 | bytes 12000000 | tf_op jit(solution)/shard_map/block/pallas_call | solution.py:561
  105.8 0.0 copy-start
  105.8 0.0 copy-start.1
  105.8 1.1 %slice_bitcast_fusion = bf16[7,2,7,7,384]{4,3,2,0,1:T(8,128)(2,1)S(1)} fusion(bf16[2,7,7,8,384]{4,3,2,1,0:T(8,128)(2,1)} %bitcast.38), kind=kLoop, calls=%fused_computation | loop fusion | bytes 1053696 | tf_op jit(solution)/shard_map/transpose | solution.py:670
  107.0 0.9 copy.40
  107.9 0.0 copy-done
  107.9 0.6 copy.59
  108.5 0.0 copy-done.1
  108.5 0.6 copy.60
  (31 shorter events, 0.2 us)
Async XLA Ops:
  105.8 2.1 %copy-start = (f32[12,576]{1,0:T(8,128)S(1)}, f32[12,576]{1,0:T(8,128)}, u32[]{:S(2)}) copy-start(f32[12,576]{1,0:T(8,128)} %get-tuple-element.13) | copy-start | bytes 82948
  105.8 2.7 %copy-start.1 = (f32[6,384]{1,0:T(8,128)S(1)}, f32[6,384]{1,0:T(8,128)}, u32[]{:S(2)}) copy-start(f32[6,384]{1,0:T(8,128)} %get-tuple-element.14) | copy-start | bytes 27652

commit v4 on v3

--- a/solution.py
+++ b/solution.py
@@ -24,7 +24,7 @@
 F32 = jnp.float32
 BF16 = jnp.bfloat16
 MESH = pl.DeviceIdType.MESH
-VMEM_LIMIT = 56 * 2**20
+VMEM_LIMIT = 58 * 2**20
 
 SIZES = (3, 7, 4)
 FIRST = (0, 3, 10)
@@ -147,12 +147,15 @@
         to = lax.rem(me + step, owners)
         return {"depth": to // heights, "height": lax.rem(to, heights)}
 
-    def member(stage, place):
-        if stage == 0:
-            return {"depth": depth // across * across + place}
-        if stage == 1:
-            return {"depth": place // heights * across + across_at, "height": lax.rem(place, heights)}
-        return {"batch": place}
+    cores = 2 - batches % 2
+    lanes = batches // cores
+    core, lane = lax.rem(batch, cores), batch // cores
+    sibling = {"batch": lane * cores + cores - 1 - core}
+    held = planes // cores
+    holder = plane_at // held == core
+
+    def lane_at(step):
+        return {"batch": lax.rem(lane + step, lanes) * cores + core}
 
     def batch_at(step):
         return {"batch": lax.rem(batch + step, batches)}
@@ -240,44 +243,131 @@
         return remote(other.at[0], other.at[0], share_send.at[batches], share_recv.at[0], before)
 
     def next_share(step):
-        return remote(other.at[0], other.at[step], share_send.at[step], share_recv.at[step], batch_at(step))
+        place = other.at[step * cores]
+        return remote(other.at[0], place, share_send.at[step], share_recv.at[step], lane_at(step))
+
+    def twin_share(step):
+        source, slot = other.at[step * cores], lanes + step
+        return remote(source, other.at[step * cores + 1], share_send.at[slot], share_recv.at[slot], sibling)
 
     def swap_merged():
         return remote(sent, fetched, merged_send.at[0], merged_recv.at[0], peer)
 
-    places = (across_at, plane_at, batch)
-    counts = (across, planes, batches)
-
-    def exchange(stage, kind, step):
-        place = lax.rem(places[stage] + step, counts[stage])
-        source = (terms[kind].at[place], partial[0][kind].at[place], partial[1][kind])[stage]
-        slot = sum(counts[:stage]) + step
-        return remote(
-            source,
-            landed[stage][kind].at[step],
-            term_send.at[kind, slot],
-            term_recv.at[kind, slot],
-            member(stage, place),
-        )
-
-    def begin(stage, kind):
-        @pl.loop(1, counts[stage])
+    paired, from_x, from_z, from_y = landed
+    chip, x_sum, z_sum, final = partial
+    base_y = across + planes
+
+    def slot_of(kind, slot):
+        return term_send.at[kind, slot], term_recv.at[kind, slot]
+
+    def to_twin(kind):
+        return remote(terms[kind].at[cores - 1 - core], paired[kind], *slot_of(kind, 0), sibling)
+
+    def to_x(kind, step):
+        place = lax.rem(across_at + step, across)
+        device = {"depth": depth // across * across + place}
+        return remote(chip[kind].at[place], from_x[kind].at[step], *slot_of(kind, step), device)
+
+    def to_z(kind, step):
+        plane = lax.rem(plane_at + step, planes)
+        device = {"depth": plane // heights * across + across_at, "height": lax.rem(plane, heights)}
+        source = x_sum[kind].at[lax.rem(plane, held)]
+        return remote(source, from_z[kind].at[step], *slot_of(kind, across + step), device)
+
+    def to_y(kind, step):
+        return remote(z_sum[kind], from_y[kind].at[step], *slot_of(kind, base_y + step), lane_at(step))
+
+    def to_other_core(kind):
+        return remote(final[kind], final[kind], *slot_of(kind, base_y), sibling)
+
+    def sends_z(step):
+        return lax.rem(plane_at + step, planes) // held == core
+
+    def begin_twin(kind):
+        if cores == 2:
+            to_twin(kind).start()
+
+    def begin_x(kind):
+        if cores == 2:
+            to_twin(kind).wait_recv()
+            chip[kind][...] = (terms[kind][core] + paired[kind][...]).astype(BF16)
+        else:
+            chip[kind][...] = terms[kind][0].astype(BF16)
+
+        @pl.loop(1, across)
         def _(step):
-            exchange(stage, kind, step).start()
-
-    def finish(stage, kind):
-        out = partial[stage][kind]
-        if stage == 0:
-            out[...] = terms[kind][across_at].astype(F32)
-        elif stage == 1:
-            out[...] = partial[0][kind][plane_at]
-        else:
-            out[...] = partial[1][kind][...]
-
-        @pl.loop(1, counts[stage])
+            to_x(kind, step).start()
+
+    def begin_z(kind):
+        x_sum[kind][...] = chip[kind][across_at].astype(F32)
+
+        @pl.loop(1, across)
         def _(step):
-            exchange(stage, kind, step).wait_recv()
-            out[...] += landed[stage][kind][step].astype(F32)
+            to_x(kind, step).wait_recv()
+            x_sum[kind][...] += from_x[kind][step].astype(F32)
+
+        @pl.loop(1, planes)
+        def _(step):
+            @pl.when(sends_z(step))
+            def _():
+                to_z(kind, step).start()
+
+    def begin_y(kind):
+        @pl.when(holder)
+        def _():
+            z_sum[kind][...] = x_sum[kind][lax.rem(plane_at, held)]
+
+            @pl.loop(1, planes)
+            def _(step):
+                to_z(kind, step).wait_recv()
+                z_sum[kind][...] += from_z[kind][step]
+
+            @pl.loop(1, lanes)
+            def _(step):
+                to_y(kind, step).start()
+
+    def begin_last(kind):
+        @pl.when(holder)
+        def _():
+            final[kind][...] = z_sum[kind][...]
+
+            @pl.loop(1, lanes)
+            def _(step):
+                to_y(kind, step).wait_recv()
+                final[kind][...] += from_y[kind][step]
+
+            if cores == 2:
+                to_other_core(kind).start()
+
+    def finish(kind):
+        if cores == 2:
+
+            @pl.when(jnp.logical_not(holder))
+            def _():
+                to_other_core(kind).wait_recv()
+
+    def settle(kind):
+        if cores == 2:
+            to_twin(kind).wait_send()
+
+        @pl.loop(1, across)
+        def _(step):
+            to_x(kind, step).wait_send()
+
+        @pl.loop(1, planes)
+        def _(step):
+            @pl.when(sends_z(step))
+            def _():
+                to_z(kind, step).wait_send()
+
+        @pl.when(holder)
+        def _():
+            @pl.loop(1, lanes)
+            def _(step):
+                to_y(kind, step).wait_send()
+
+            if cores == 2:
+                to_other_core(kind).wait_send()
 
     barrier = pltpu.get_barrier_semaphore()
 
@@ -362,7 +452,7 @@
         def _():
             pass_on(DEEP[1])
 
-        @pl.when(turn == 3 + 2 * late)
+        @pl.when(turn == 2 + 2 * late)
         def _():
             first_share().wait_recv()
 
@@ -370,7 +460,10 @@
             def _():
                 pass_share().start()
 
-            @pl.loop(1, batches)
+            if cores == 2:
+                twin_share(0).start()
+
+            @pl.loop(1, lanes)
             def _(step):
                 next_share(step).start()
 
@@ -411,13 +504,20 @@
                                 back(zone, half).start()
 
     def place_of(owner):
-        return owner // heights % across, owner // heights // across * heights + owner % heights
+        plane = owner // heights // across * heights + owner % heights
+        return plane // held, owner // heights % across, plane % held
 
     spread = jnp.transpose(grad[...])
     terms[0][...] = jnp.zeros_like(terms[0])
     for o in range(owners):
-        terms[0][*place_of(o), 0:lines, 0 : 3 * ATTN] = spread[o * lines : (o + 1) * lines].astype(BF16)
-    begin(0, 0)
+        terms[0][*place_of(o), 0:lines, 0 : 3 * ATTN] = spread[o * lines : (o + 1) * lines]
+    begin_twin(0)
+
+    @pl.loop(1, lanes)
+    def _(step):
+        next_share(step).wait_recv()
+        if cores == 2:
+            twin_share(step).start()
 
     for zone in ZONES:
         if zone not in AHEAD:
@@ -444,15 +544,17 @@
                 for half in range(2):
                     back(zone, half).wait_recv()
         restore(dz)
+        if dz == 1:
+            begin_x(0)
 
     grad_proj = tn(context_all[...], pad_u[...].reshape(EDGE * SLAB, C))
     terms[1][...] = jnp.zeros_like(terms[1])
     per = ATTN // owners
     for o in range(owners):
-        rows = grad_proj[o * per : (o + 1) * per].astype(BF16)
+        rows = grad_proj[o * per : (o + 1) * per]
         terms[1][*place_of(o), 0:per, 0:ATTN] = rows[:, 0:ATTN]
         terms[1][*place_of(o), per : 2 * per, 0:ATTN] = rows[:, ATTN:]
-    begin(0, 1)
+    begin_twin(1)
 
     def merge_pair(pair):
         blocks = []
@@ -471,44 +573,45 @@
         for o in range(8):
             features[o, pair * 56 : pair * 56 + 56, :] = centered[o] * factor * params[2 + o : 3 + o, :]
 
-    for pair in range(4):
+    for pair in range(EDGE // 2):
         merge_pair(pair)
-    finish(0, 0)
-    begin(1, 0)
-    for pair in range(4, EDGE // 2):
-        merge_pair(pair)
-    finish(0, 1)
-    begin(1, 1)
-
-    @pl.loop(1, batches)
-    def _(step):
-        next_share(step).wait_recv()
+        if pair == 1:
+            begin_x(1)
+        if pair == 4:
+            begin_z(0)
+    begin_z(1)
+    if cores == 2:
+
+        @pl.loop(0, lanes)
+        def _(step):
+            twin_share(step).wait_recv()
 
     each = 8 // batches
     result = jnp.zeros(features.shape[1:], F32)
     for step in range(batches):
-        at = lax.rem(batch - step + batches, batches) * each
+        crop = lax.rem(lane - step // cores + lanes, lanes) * cores
+        at = (crop + (core if step % cores == 0 else cores - 1 - core)) * each
         for k in range(each):
             result += nn(features[at + k].astype(BF16), other[step, k * C : (k + 1) * C, :])
     sent[0 : result.shape[0], :] = result.astype(BF16)
     sent[result.shape[0] :, :] = jnp.zeros((sent.shape[0] - result.shape[0], C), BF16)
     swap_merged().start()
-    for kind in range(2):
-        finish(1, kind)
-        begin(2, kind)
+    begin_y(0)
+    begin_y(1)
     result = jnp.zeros(features.shape[1:], F32)
     for step in range(batches):
         for k in range(each):
             result += nn(features[step * each + k].astype(BF16), own[step, k * C : (k + 1) * C, :])
     merged_out[height] = result.astype(BF16)
-    for kind in range(2):
-        finish(2, kind)
-    sums = partial[2]
-    grad_qkv_out[...] = sums[0][0:lines, 0 : 3 * ATTN]
-    grad_proj_out[:, 0:ATTN] = sums[1][0:per, 0:ATTN]
-    grad_proj_out[:, ATTN:] = sums[1][per : 2 * per, 0:ATTN]
+    begin_last(0)
+    begin_last(1)
     swap_merged().wait_recv()
     merged_out[heights - 1 - height] = fetched[0 : result.shape[0], :]
+    finish(0)
+    finish(1)
+    grad_qkv_out[...] = final[0][0:lines, 0 : 3 * ATTN]
+    grad_proj_out[:, 0:ATTN] = final[1][0:per, 0:ATTN]
+    grad_proj_out[:, ATTN:] = final[1][per : 2 * per, 0:ATTN]
 
     for zone in HALO:
         for half in range(2):
@@ -531,16 +634,18 @@
 
     swap_merged().wait_send()
 
-    @pl.loop(1, batches)
+    @pl.loop(1, lanes)
     def _(step):
         next_share(step).wait_send()
 
-    for stage in range(3):
-        for kind in range(2):
-
-            @pl.loop(1, counts[stage])
-            def _(step):
-                exchange(stage, kind, step).wait_send()
+    if cores == 2:
+
+        @pl.loop(0, lanes)
+        def _(step):
+            twin_share(step).wait_send()
+
+    settle(0)
+    settle(1)
 
 
 def run_block(operands, sizes):
@@ -556,7 +661,9 @@
     def pair_of(kind, *shape):
         return [pltpu.VMEM(shape + (lines, wide), kind), pltpu.VMEM(shape + (lines, narrow), kind)]
 
-    exchanges = across + planes + batches
+    cores = 2 - batches % 2
+    held = planes // cores
+    exchanges = across + planes + batches // cores
 
     return pl.pallas_call(
         functools.partial(block_kernel, sizes),
@@ -587,9 +694,14 @@
             pltpu.VMEM((batches, 8 * C // batches, C), BF16),
             pltpu.VMEM((up(cell_rows, 16), C), BF16),
             pltpu.VMEM((up(cell_rows, 16), C), BF16),
-            pair_of(BF16, across, planes),
-            [pair_of(BF16, across, planes), pair_of(F32, planes), pair_of(F32, batches)],
-            [pair_of(F32, planes), pair_of(F32), pair_of(F32)],
+            pair_of(F32, cores, across, held),
+            [
+                pair_of(F32, across, held),
+                pair_of(BF16, across, held),
+                pair_of(F32, planes),
+                pair_of(F32, batches // cores),
+            ],
+            [pair_of(BF16, across, held), pair_of(F32, held), pair_of(F32), pair_of(F32)],
             pltpu.SemaphoreType.DMA((10,)),
             pltpu.SemaphoreType.DMA((10,)),
             pltpu.SemaphoreType.DMA((10,)),

time: 109 us -> 107 us (0.982)
  Pallas kernels: 97.7 us -> 94.9 us
    pallas_call x1, Pallas kernels: 97.7 us -> 94.9 us  [run_block(): pl.pallas_call(functools.partial(block_kernel, sizes), out_shape=[jax.Sha...]
where the time goes in v4:
time: 107 us; the launch traced here: 106 us
  Pallas kernels  94.9 us (89%)
  local copies, waits for them, and re-layouts  7.3 us (7%)
  other arithmetic  3.24 us (3%)
    pallas_call x1, Pallas kernels, run_block(): pl.pallas_call(functools.partial(block_kernel, sizes), out_shape=[jax.Sha...  94.9 us

profile of v4, /device:TPU:1, one launch (start us, length us, event | category | flops | bytes accessed | tf_op | source)
XLA Modules:
  0.0 106.4 jit_solution(6950853009205058320)
XLA Ops:
  0.6 0.7 convert_element_type.39
  1.3 0.7 pad_maximum_fusion
  2.0 0.6 reshape.112.refs_7_
  2.6 1.0 convert.5
  3.7 0.7 convert_element_type.40.refs_2_
  4.4 0.9 copy.50
  5.3 0.1 reshape.110
  5.4 0.1 reshape.111
  5.5 0.1 reshape.108
  5.6 0.1 reshape.109
  5.7 0.1 reshape.106
  5.8 0.1 reshape.107
  5.9 0.1 reshape.104
  6.0 0.1 reshape.105
  6.1 0.1 fusion.2
  6.2 0.1 reshape.102
  6.3 0.1 reshape.103
  6.4 0.1 reshape.98
  6.5 0.1 reshape.99
  6.6 0.1 reshape.96
  6.7 0.1 reshape.97
  6.8 0.1 select_add_fusion.1
  7.0 0.1 reshape.100
  7.1 0.1 reshape.101
  7.2 0.1 select_add_fusion
  7.3 0.1 reshape.94
  7.4 0.1 reshape.95
  7.5 0.6 pad_maximum_fusion.1.refs_3_
  8.1 94.9 %block.1 = (bf16[2,392,384]{2,1,0:T(8,128)(2,1)}, f32[12,576]{1,0:T(8,128)}, f32[6,384]{1,0:T(8,128)}) custom-call(bf16[1,14,14,14,384]{4,3,2,1,0:T(8,128)(2,1)} %refs_0_.1, bf16[1,14,14,14,384]{4,3,2,1,0:T(8,128)(2,1)} %refs_1_.1, bf16[14,1,224]{2,1,0:T(2,128)(2,1)} %convert_element_type.40.refs_2_, f32[8,1,384]{2,1,0:T(1,128)} %pad_maximum_fusion.1.refs_3_, ...), custom_call_target="tpu_custom_call" | custom-call | flops 80000000000 | bytes 12000000 | tf_op jit(solution)/shard_map/block/pallas_call | solution.py:668
  103.1 0.0 copy-start
  103.1 0.0 copy-start.1
  103.1 1.1 %slice_bitcast_fusion = bf16[7,2,7,7,384]{4,3,2,0,1:T(8,128)(2,1)S(1)} fusion(bf16[2,7,7,8,384]{4,3,2,1,0:T(8,128)(2,1)} %bitcast.38), kind=kLoop, calls=%fused_computation | loop fusion | bytes 1053696 | tf_op jit(solution)/shard_map/transpose | solution.py:782
  104.3 0.9 copy.40
  105.1 0.0 copy-done
  105.1 0.6 copy.59
  105.8 0.0 copy-done.1
  105.8 0.6 copy.60
  (31 shorter events, 0.2 us)
Async XLA Ops:
  103.1 2.1 %copy-start = (f32[12,576]{1,0:T(8,128)S(1)}, f32[12,576]{1,0:T(8,128)}, u32[]{:S(2)}) copy-start(f32[12,576]{1,0:T(8,128)} %get-tuple-element.13) | copy-start | bytes 82948
  103.1 2.7 %copy-start.1 = (f32[6,384]{1,0:T(8,128)S(1)}, f32[6,384]{1,0:T(8,128)}, u32[]{:S(2)}) copy-start(f32[6,384]{1,0:T(8,128)} %get-tuple-element.14) | copy-start | bytes 27652

commit v5 on v4

--- a/solution.py
+++ b/solution.py
@@ -102,7 +102,7 @@
             AHEAD[zone] = (_group, _row)
         _row += ZONE_ROWS[zone]
 HALO = list(AHEAD)
-DEEP = [(0, 1), (0, 2)]
+DEEP = {((0, 1), 0): 1, ((0, 1), 1): 3, ((0, 2), 0): 2}
 LATER = [(2, 0), (0, 2), (0, 0)]
 GROUP_LIST = list(GROUPS)
 
@@ -132,7 +132,7 @@
     share_send, share_recv, merged_send, merged_recv, term_send, term_recv = refs[41:47]
     send_buffers = dict(zip(HALO, refs[47:52]))
     score_all, weight_all, dscore_all, weight, relay_send, relay_recv = refs[52:58]
-    relay_buffers = dict(zip(DEEP, refs[58:60]))
+    relay_buffers = dict(zip(DEEP, refs[58:61]))
 
     depth, height, batch = (lax.axis_index(n) for n in ("depth", "height", "batch"))
     me = depth * heights + height
@@ -183,46 +183,48 @@
             neighbour(zone, -1, sizes),
         )
 
-    def to_relay(zone):
-        slot = DEEP.index(zone)
+    def to_relay(piece):
+        zone, half = piece
         return remote(
-            send_buffers[zone].at[1],
-            relay_buffers[zone],
-            ahead_send.at[2 * HALO.index(zone) + 1],
-            relay_recv.at[slot],
-            {"depth": lax.rem(depth + 3, depths)},
+            send_buffers[zone].at[half],
+            relay_buffers[piece],
+            ahead_send.at[2 * HALO.index(zone) + half],
+            relay_recv.at[list(DEEP).index(piece)],
+            {"depth": lax.rem(depth + DEEP[piece], depths)},
         )
 
-    def from_relay(zone):
+    def from_relay(piece):
+        zone, half = piece
         return remote(
-            relay_buffers[zone],
-            landing(zone, 1),
-            relay_send.at[DEEP.index(zone)],
-            ahead_recv.at[2 * HALO.index(zone) + 1],
-            {"depth": lax.rem(depth + depths - 4, depths)},
+            relay_buffers[piece],
+            landing(zone, half),
+            relay_send.at[list(DEEP).index(piece)],
+            ahead_recv.at[2 * HALO.index(zone) + half],
+            {"depth": lax.rem(depth + depths - 1 - DEEP[piece], depths)},
         )
 
     def send_ahead(zone):
-        ahead(zone, 0).start()
-        if relayed and zone in DEEP:
-
-            @pl.when(late == 1)
-            def _():
-                to_relay(zone).start()
-
-            @pl.when(late == 0)
-            def _():
-                ahead(zone, 1).start()
-        else:
-            ahead(zone, 1).start()
+        for half in range(2):
+            if relayed and (zone, half) in DEEP:
+
+                @pl.when(late == 1)
+                def _():
+                    to_relay((zone, half)).start()
+
+                @pl.when(late == 0)
+                def _():
+                    ahead(zone, half).start()
+            else:
+                ahead(zone, half).start()
 
     def pass_on(zone):
-        if relayed:
-
-            @pl.when(along == 3)
-            def _():
-                to_relay(zone).wait_recv()
-                from_relay(zone).start()
+        for piece, place in DEEP.items():
+            if relayed and piece[0] == zone:
+
+                @pl.when(along == place)
+                def _():
+                    to_relay(piece).wait_recv()
+                    from_relay(piece).start()
 
     def back(zone, half):
         group, row = AHEAD[zone]
@@ -441,7 +443,7 @@
 
         @pl.when(turn == 0)
         def _():
-            pass_on(DEEP[0])
+            pass_on((0, 1))
 
         @pl.when(turn == 1)
         def _():
@@ -450,7 +452,7 @@
 
         @pl.when(turn == 3)
         def _():
-            pass_on(DEEP[1])
+            pass_on((0, 2))
 
         @pl.when(turn == 2 + 2 * late)
         def _():
@@ -619,10 +621,11 @@
             back(zone, half).wait_send()
     if relayed:
 
-        @pl.when(along == 3)
-        def _():
-            for zone in DEEP:
-                from_relay(zone).wait_send()
+        for piece, place in DEEP.items():
+
+            @pl.when(along == place)
+            def _():
+                from_relay(piece).wait_send()
 
     @pl.when(late == 0)
     def _():
@@ -719,10 +722,10 @@
             pltpu.VMEM((HEADS, ROWS, ROWS), BF16),
             pltpu.VMEM((HEADS, ROWS, ROWS), BF16),
             pltpu.VMEM((C, 3 * ATTN), BF16),
-            pltpu.SemaphoreType.DMA((2,)),
-            pltpu.SemaphoreType.DMA((2,)),
+            pltpu.SemaphoreType.DMA((3,)),
+            pltpu.SemaphoreType.DMA((3,)),
         ]
-        + [pltpu.VMEM((ZONE_ROWS[zone], FEED), BF16) for zone in DEEP],
+        + [pltpu.VMEM((ZONE_ROWS[zone], FEED), BF16) for zone, _ in DEEP],
         cost_estimate=pl.CostEstimate(flops=80_000_000_000, bytes_accessed=12_000_000, transcendentals=8_000_000),
         compiler_params=pltpu.CompilerParams(
             collective_id=1, has_side_effects=True, vmem_limit_bytes=VMEM_LIMIT

time: 107 us -> 105 us (0.981)
  Pallas kernels: 94.9 us -> 93.5 us
    pallas_call x1, Pallas kernels: 94.9 us -> 93.5 us  [run_block(): pl.pallas_call(functools.partial(block_kernel, sizes), out_shape=[jax.Sha...]
where the time goes in v5:
time: 105 us
  Pallas kernels  93.5 us (89%)
  local copies, waits for them, and re-layouts  7.3 us (7%)
  other arithmetic  3.24 us (3%)
    pallas_call x1, Pallas kernels, run_block(): pl.pallas_call(functools.partial(block_kernel, sizes), out_shape=[jax.Sha...  93.5 us
    unnamed x8, local copies, waits for them, and re-layouts  2.14 us

profile of v5, /device:TPU:1, one launch (start us, length us, event | category | flops | bytes accessed | tf_op | source)
XLA Modules:
  0.0 105.0 jit_solution(5584142453545679792)
XLA Ops:
  0.6 0.7 convert_element_type.39
  1.3 0.7 pad_maximum_fusion
  2.0 0.6 reshape.112.refs_7_
  2.6 1.0 convert.5
  3.7 0.7 convert_element_type.40.refs_2_
  4.4 0.9 copy.50
  5.3 0.1 reshape.110
  5.4 0.1 reshape.111
  5.5 0.1 reshape.108
  5.6 0.1 reshape.109
  5.7 0.1 reshape.106
  5.8 0.1 reshape.107
  5.9 0.1 reshape.104
  6.0 0.1 reshape.105
  6.1 0.1 fusion.2
  6.2 0.1 reshape.102
  6.3 0.1 reshape.103
  6.4 0.1 reshape.98
  6.5 0.1 reshape.99
  6.6 0.1 reshape.96
  6.7 0.1 reshape.97
  6.8 0.1 select_add_fusion.1
  7.0 0.1 reshape.100
  7.1 0.1 reshape.101
  7.2 0.1 select_add_fusion
  7.3 0.1 reshape.94
  7.4 0.1 reshape.95
  7.5 0.6 pad_maximum_fusion.1.refs_3_
  8.1 93.5 %block.1 = (bf16[2,392,384]{2,1,0:T(8,128)(2,1)}, f32[12,576]{1,0:T(8,128)}, f32[6,384]{1,0:T(8,128)}) custom-call(bf16[1,14,14,14,384]{4,3,2,1,0:T(8,128)(2,1)} %refs_0_.1, bf16[1,14,14,14,384]{4,3,2,1,0:T(8,128)(2,1)} %refs_1_.1, bf16[14,1,224]{2,1,0:T(2,128)(2,1)} %convert_element_type.40.refs_2_, f32[8,1,384]{2,1,0:T(1,128)} %pad_maximum_fusion.1.refs_3_, ...), custom_call_target="tpu_custom_call" | custom-call | flops 80000000000 | bytes 12000000 | tf_op jit(solution)/shard_map/block/pallas_call | solution.py:671
  101.7 0.0 copy-start
  101.7 0.0 copy-start.1
  101.7 1.1 %slice_bitcast_fusion = bf16[7,2,7,7,384]{4,3,2,0,1:T(8,128)(2,1)S(1)} fusion(bf16[2,7,7,8,384]{4,3,2,1,0:T(8,128)(2,1)} %bitcast.38), kind=kLoop, calls=%fused_computation | loop fusion | bytes 1053696 | tf_op jit(solution)/shard_map/transpose | solution.py:785
  102.9 0.9 copy.40
  103.7 0.0 copy-done
  103.7 0.6 copy.59
  104.4 0.0 copy-done.1
  104.4 0.6 copy.60
  (31 shorter events, 0.2 us)
Async XLA Ops:
  101.7 2.1 %copy-start = (f32[12,576]{1,0:T(8,128)S(1)}, f32[12,576]{1,0:T(8,128)}, u32[]{:S(2)}) copy-start(f32[12,576]{1,0:T(8,128)} %get-tuple-element.13) | copy-start | bytes 82948
  101.7 2.7 %copy-start.1 = (f32[6,384]{1,0:T(8,128)S(1)}, f32[6,384]{1,0:T(8,128)}, u32[]{:S(2)}) copy-start(f32[6,384]{1,0:T(8,128)} %get-tuple-element.14) | copy-start | bytes 27652
